TPU v7x, 32 devices: a whole 2x2x4 slice. The times are simulated.
32 devices in a mesh: parts: 2 (over x), grid: 8 (over z, y), depth: 2 (over core).
Axes of the slice: x: 2, y: 2, z: 4, core: 2. Of those that a mesh axis runs over, the one named last changes fastest.
Arguments:
- gate_input: bfloat16 [1024, 32768], P(('parts', 'depth'), 'grid'), parts along dimension 0, may hold values from -6 to 6
- up_input: bfloat16 [1024, 32768], P(('parts', 'depth'), 'grid'), parts along dimension 0, may hold values from -6 to 6
- code_values: bfloat16 [32768, 8192], P('grid', 'depth'), may hold values from -6 to 6, as said below
- exponents: int32 [1024, 8192], P('grid', 'depth'), may hold values from -10 to -7
- cotangent: bfloat16 [1024, 8192], P(('parts', 'depth'), 'grid'), parts along dimension 0, may hold values from -1.5 to 1.5
Outputs:
- output_rows: bfloat16 [1024, 8192], P(('parts', 'depth'), 'grid'), parts along dimension 0
- grad_gate: bfloat16 [1024, 32768], P(('parts', 'depth'), 'grid'), parts along dimension 0
- grad_up: bfloat16 [1024, 32768], P(('parts', 'depth'), 'grid'), parts along dimension 0
- grad_weight: bfloat16 [65536, 8192], P(('parts', 'grid'), 'depth'), parts along dimension 0
There are 2 independent parts, one for each index of `parts`. A program takes and returns all parts, laid end to end along the dimension named above; an argument that names none is the same for every part. Nothing has to cross between parts.
Inputs may be any that keep to these rules, and one draw needn't show every extreme that they name: `code_values`: every entry is one of the E2M1 values 0, +-0.5, +-1, +-1.5, +-2, +-3, +-4, +-6.
All inputs are finite; a program needn't handle non-finite values.
Results may differ from a plain program's by a relative error of at most 0.0049.
Values may be sent and summed in bfloat16 or wider, within the bound.
No kernel may reach another device: no remote copies, remote signals or barrier semaphores. Data moves between devices by JAX's collectives and lax.ppermute only.
A program may use at most 448 MiB of HBM per device.

v0:
```python
import functools

import jax
import jax.numpy as jnp
from jax import lax
from jax.experimental import pallas as pl
from jax.experimental.pallas import tpu as pltpu
from jax.sharding import PartitionSpec as P

F32 = jnp.float32
BF16 = jnp.bfloat16
VMEM_BYTES = 30 * 1024 * 1024
SWAP = [(0, 1), (1, 0)]
ANY = pl.BlockSpec(memory_space=pl.ANY)


def params(size=VMEM_BYTES):
    return pltpu.CompilerParams(vmem_limit_bytes=size)


def cost(flops, size):
    return pl.CostEstimate(flops=flops, bytes_accessed=size, transcendentals=0)


def dequantize(codes, exponents):
    rows, columns = codes.shape
    scale = jnp.exp2(exponents.astype(F32)).astype(BF16)
    blocks = codes.reshape(rows // 32, 32, columns) * scale.reshape(rows // 32, 1, columns)
    return blocks.reshape(rows, columns)


def sigmoid(value):
    return 0.5 * jnp.tanh(0.5 * value) + 0.5


def make_hidden(gate, up):
    tokens, units = gate.shape
    tile = min(units, 1024)
    tiles = units // tile

    def body(g_ref, u_ref, h_ref, gate_held, up_held, out_held, in_sem, out_sem):
        def columns(i):
            return pl.ds(i * tile, tile)

        def store(i):
            return pltpu.make_async_copy(out_held.at[i], h_ref.at[:, columns(i)], out_sem.at[i])

        for i in range(tiles):
            pltpu.make_async_copy(g_ref.at[:, columns(i)], gate_held.at[i], in_sem.at[i, 0]).start()
            pltpu.make_async_copy(u_ref.at[:, columns(i)], up_held.at[i], in_sem.at[i, 1]).start()
        for i in range(tiles):
            wait(gate_held.at[i], in_sem.at[i, 0])
            wait(up_held.at[i], in_sem.at[i, 1])
            value = gate_held[i].astype(F32)
            out_held[i] = (value * sigmoid(value) * up_held[i].astype(F32)).astype(BF16)
            store(i).start()
        for i in range(tiles):
            store(i).wait()

    held = pltpu.VMEM((tiles, tokens, tile), BF16)
    return pl.pallas_call(
        body,
        in_specs=[ANY] * 2,
        out_specs=ANY,
        out_shape=jax.ShapeDtypeStruct((tokens, units), BF16),
        scratch_shapes=[held, held, held, pltpu.SemaphoreType.DMA((tiles, 2)), pltpu.SemaphoreType.DMA((tiles,))],
        compiler_params=params(60 * 1024 * 1024),
        cost_estimate=cost(10 * tokens * units, 6 * tokens * units),
    )(gate, up)


def finish(gate, up, mine, other, first, so_far, *deps):
    tokens, units = gate.shape
    width = mine.shape[1]
    tile = min(width, 1024)
    base = first // tile

    def body(g_ref, u_ref, m_ref, o_ref, *refs):
        dg_ref, du_ref = refs[-2:]
        value = g_ref[...].astype(F32)
        s = sigmoid(value)
        grad = m_ref[...] + o_ref[...].astype(F32)
        slope = s * (1.0 + value * (1.0 - s))
        dg_ref[...] = (grad * u_ref[...].astype(F32) * slope).astype(BF16)
        du_ref[...] = (grad * (value * s)).astype(BF16)

    there = pl.BlockSpec((tokens, tile), lambda i: (0, base + i))
    here = pl.BlockSpec((tokens, tile), lambda i: (0, i))
    shape = jax.ShapeDtypeStruct((tokens, units), BF16)
    return pl.pallas_call(
        body,
        grid=(width // tile,),
        in_specs=[there, there, here, here] + [ANY] * (len(so_far) + len(deps)),
        out_specs=[there] * 2,
        out_shape=[shape] * 2,
        input_output_aliases={4: 0, 5: 1} if so_far else {},
        compiler_params=params(),
        cost_estimate=cost(20000 * tokens * width, 1000 * tokens * width),
    )(gate, up, mine, other, *so_far, *deps)


def block(i, size):
    return pl.ds(pl.multiple_of(i * size, size), size)


def wait(ref, semaphore):
    pltpu.make_async_copy(ref, ref, semaphore).wait()


def output_terms(places, hidden, hidden_other, codes, exponents, part, deps=(), turn=False):
    tokens, units = hidden.shape
    tile = min(part, 512)
    step = min(units, 1024)
    count = places.shape[0]
    tiles = part // tile
    last = count * tiles
    steps = range(0, units, step)
    outputs = 3 if turn else 2

    def body(p_ref, h_ref, x_ref, c_ref, e_ref, *refs):
        out = refs[len(deps) : len(deps) + outputs]
        held, codes_held, exponents_held, out_held, h_sem, c_sem, e_sem, o_sem, *more = refs[len(deps) + outputs :]

        def columns(i):
            return block(p_ref[i // tiles] * tiles + i % tiles, tile)

        def fetch(i, rows, semaphore):
            pltpu.make_async_copy(c_ref.at[rows, columns(i)], codes_held.at[i % 2, rows], semaphore).start()

        def fetch_exponents(i):
            pltpu.make_async_copy(e_ref.at[:, columns(i)], exponents_held.at[i % 2], e_sem.at[i % 2]).start()

        def stores(i):
            rows, lanes = block(i // tiles, tokens), block(i % tiles, tile)
            return [
                pltpu.make_async_copy(out_held.at[i % 2, :tokens], out[0].at[rows, lanes], o_sem.at[i % 2, 0]),
                pltpu.make_async_copy(out_held.at[i % 2, tokens:], out[1].at[rows, lanes], o_sem.at[i % 2, 1]),
            ]

        fetch_exponents(0)
        for n, k in enumerate(steps):
            rows = pl.ds(k, step)
            pltpu.make_async_copy(h_ref.at[:, rows], held.at[:tokens, rows], h_sem.at[n]).start()
            pltpu.make_async_copy(x_ref.at[:, rows], held.at[tokens:, rows], h_sem.at[n]).start()
            fetch(0, rows, c_sem.at[n])
        if last > 1:
            fetch_exponents(1)
            fetch(1, pl.ds(0, units), c_sem.at[len(steps)])

        def work(i):
            wait(exponents_held.at[i % 2], e_sem.at[i % 2])
            total = None
            for n, k in enumerate(steps):
                rows = pl.ds(k, step)
                if isinstance(i, int):
                    wait(held.at[:, rows], h_sem.at[n])
                    wait(codes_held.at[0, rows], c_sem.at[n])
                weight = dequantize(codes_held[i % 2, rows], exponents_held[i % 2, k // 32 : (k + step) // 32, :])
                term = jnp.dot(held[:, rows], weight, preferred_element_type=F32)
                total = term if total is None else total + term
                if turn and isinstance(i, int):
                    turned_held, t_sem = more
                    turned_held[rows] = held[:, rows].T
                    pltpu.make_async_copy(turned_held.at[rows], out[2].at[rows], t_sem.at[n]).start()
            return total.astype(BF16)

        def go_on(i):
            for copy in stores(i):
                copy.start()

            @pl.when(i + 2 < last)
            def _():
                fetch_exponents(i + 2)
                fetch(i + 2, pl.ds(0, units), c_sem.at[len(steps) + (i + 1) % 2])

        out_held[0] = work(0)
        go_on(0)

        @pl.loop(1, last)
        def _(i):
            wait(codes_held.at[i % 2], c_sem.at[len(steps) + (i + 1) % 2])
            total = work(i)

            @pl.when(i >= 2)
            def _():
                for copy in stores(i - 2):
                    copy.wait()

            out_held[i % 2] = total
            go_on(i)

        for i in range(max(0, last - 2), last):
            for copy in stores(i):
                copy.wait()
        if turn:
            turned_held, t_sem = more
            for n, k in enumerate(steps):
                wait(turned_held.at[pl.ds(k, step)], t_sem.at[n])

    out = pl.pallas_call(
        body,
        in_specs=[pl.BlockSpec(memory_space=pltpu.SMEM)] + [ANY] * (4 + len(deps)),
        out_specs=[ANY] * outputs,
        out_shape=[jax.ShapeDtypeStruct((count * tokens, part), BF16)] * 2
        + ([jax.ShapeDtypeStruct((units, 2 * tokens), BF16)] if turn else []),
        scratch_shapes=[
            pltpu.VMEM((2 * tokens, units), BF16),
            pltpu.VMEM((2, units, tile), BF16),
            pltpu.VMEM((2, units // 32, tile), jnp.int32),
            pltpu.VMEM((2, 2 * tokens, tile), BF16),
            pltpu.SemaphoreType.DMA((len(steps),)),
            pltpu.SemaphoreType.DMA((len(steps) + 2,)),
            pltpu.SemaphoreType.DMA((2,)),
            pltpu.SemaphoreType.DMA((2, 2)),
        ]
        + ([pltpu.VMEM((units, 2 * tokens), BF16), pltpu.SemaphoreType.DMA((len(steps),))] if turn else []),
        compiler_params=params(),
        cost_estimate=cost(4 * tokens * units * part * count, 2 * units * part * count),
    )(places, hidden, hidden_other, codes, exponents, *deps)
    return out


class Slots:
    def __init__(self, blocks):
        self.blocks = blocks
        self.arrays = [piece[0] for block in blocks for rows in block for piece in rows]
        self.tokens = sum(piece[2] for piece in blocks[0][2])
        self.part = blocks[0][2][0][0].shape[1]

    def scratch(self):
        return [
            pltpu.VMEM((len(self.blocks), 2 * self.tokens, self.part), BF16),
            pltpu.SemaphoreType.DMA((len(self.blocks),)),
        ]

    def load(self, j, flags, refs, held, semaphores):
        before = sum(len(rows) for block in self.blocks[:j] for rows in block)
        refs = iter(refs[before:])
        for wanted, rows in zip((1, 0, None), self.blocks[j]):
            copies, row = [], self.tokens if wanted is None else 0
            for _, first, size in rows:
                copies.append(
                    pltpu.make_async_copy(
                        next(refs).at[pl.ds(first, size)], held.at[j, pl.ds(row, size)], semaphores.at[j]
                    )
                )
                row += size

            def start(copies=copies):
                for copy in copies:
                    copy.start()

            if wanted is None:
                start()
            else:
                pl.when(flags[j] == wanted)(start)


def run(phases, deps=(), size=VMEM_BYTES):
    smem = pl.BlockSpec(memory_space=pltpu.SMEM)
    ends = []
    aliases = {}
    given, made, held = 0, 0, 0
    for phase in phases:
        for i, o in phase["aliases"].items():
            aliases[given + i] = made + o
        ends.append((given, made, held))
        given += phase["scalars"] + len(phase["inputs"])
        made += len(phase["shapes"])
        held += len(phase["scratch"])
    ends.append((given, made, held))

    def body(*refs):
        inputs, outputs = refs[:given], refs[given + len(deps) : given + len(deps) + made]
        scratch = refs[given + len(deps) + made :]
        steps = []
        for phase, (i, o, h), (i_end, o_end, h_end) in zip(phases, ends, ends[1:]):
            steps.append(phase["body"](*inputs[i:i_end], *outputs[o:o_end], *scratch[h:h_end]))
        for step in steps:
            next(step)
        for step in steps:
            next(step, None)

    out = pl.pallas_call(
        body,
        in_specs=[
            spec for p in phases for spec in [smem] * p["scalars"] + [ANY] * len(p["inputs"])
        ]
        + [ANY] * len(deps),
        out_specs=[ANY] * made,
        out_shape=[shape for p in phases for shape in p["shapes"]],
        input_output_aliases=aliases,
        scratch_shapes=[shape for p in phases for shape in p["scratch"]],
        compiler_params=params(size),
        cost_estimate=cost(sum(p["flops"] for p in phases), sum(p["size"] for p in phases)),
    )(*[value for p in phases for value in p["numbers"] + p["inputs"]], *deps)
    return [out[a[1] : b[1]] for a, b in zip(ends, ends[1:])]


def hidden_gradient(places, flags, slots, codes, exponents, first, width, alone=True):
    tokens, part, count = slots.tokens, slots.part, len(slots.blocks)
    tile = min(width, 512)
    tiles = width // tile
    given = len(slots.arrays)
    step = min(part, 1024)

    def body(p_ref, f_ref, *refs):
        c_ref, e_ref = refs[given : given + 2]
        m_ref, o_ref, held, t_sem, codes_held, exponents_held, m_held, o_held, c_sem, e_sem, o_sem = refs[given + 2 :]

        def columns(j):
            return pl.ds(pl.multiple_of(p_ref[j] * part, part), part)

        def fetch(i, j):
            rows = pl.ds(first + pl.multiple_of(i * tile, tile), tile)
            pltpu.make_async_copy(c_ref.at[rows, columns(j)], codes_held.at[i % 2, j], c_sem.at[i % 2, j]).start()

        def stores(i):
            lanes = block(i, tile)
            return [
                pltpu.make_async_copy(m_held.at[i % 2], m_ref.at[:, lanes], o_sem.at[i % 2, 0]),
                pltpu.make_async_copy(o_held.at[i % 2], o_ref.at[:, lanes], o_sem.at[i % 2, 1]),
            ]

        for j in range(count):
            slots.load(j, f_ref, refs[:given], held, t_sem)
            fetch(0, j)
            rows = pl.ds(first // 32, width // 32)
            pltpu.make_async_copy(e_ref.at[rows, columns(j)], exponents_held.at[j], e_sem.at[j]).start()
        if tiles > 1:
            for j in range(count):
                fetch(1, j)
        yield

        def arrive(j):
            wait(held.at[j], t_sem.at[j])
            wait(exponents_held.at[j], e_sem.at[j])

        def work(i, step_by_step):
            if not step_by_step:
                for j in range(count):
                    wait(codes_held.at[i % 2, j], c_sem.at[i % 2, j])
            total = None
            for j in range(count):
                if step_by_step:
                    arrive(j)
                    wait(codes_held.at[i % 2, j], c_sem.at[i % 2, j])
                for k in range(0, part, step):
                    lanes = pl.ds(k, step)
                    weight = dequantize(
                        codes_held[i % 2, j, :, lanes], exponents_held[j, block(i, tile // 32), lanes]
                    )
                    term = lax.dot_general(
                        held[j, :, lanes], weight, (((1,), (1,)), ((), ())), preferred_element_type=F32
                    )
                    total = term if total is None else total + term

            @pl.when(i >= 2)
            def _():
                for copy in stores(i - 2):
                    copy.wait()

            m_held[i % 2] = total[:tokens]
            o_held[i % 2] = total[tokens:].astype(BF16)
            for copy in stores(i):
                copy.start()

            @pl.when(i + 2 < tiles)
            def _():
                for j in range(count):
                    fetch(i + 2, j)

        if alone:
            work(0, True)
        else:
            for j in range(count):
                arrive(j)

        @pl.loop(1 if alone else 0, tiles)
        def _(i):
            work(i, False)

        for i in range(max(0, tiles - 2), tiles):
            for copy in stores(i):
                copy.wait()

    return dict(
        body=body,
        scalars=2,
        numbers=[places, flags],
        inputs=[*slots.arrays, codes, exponents],
        shapes=[jax.ShapeDtypeStruct((tokens, width), F32), jax.ShapeDtypeStruct((tokens, width), BF16)],
        aliases={},
        scratch=slots.scratch()
        + [
            pltpu.VMEM((2, count, tile, part), BF16),
            pltpu.VMEM((count, width // 32, part), jnp.int32),
            pltpu.VMEM((2, tokens, tile), F32),
            pltpu.VMEM((2, tokens, tile), BF16),
            pltpu.SemaphoreType.DMA((2, count)),
            pltpu.SemaphoreType.DMA((count,)),
            pltpu.SemaphoreType.DMA((2, 2)),
        ],
        flops=4 * tokens * width * part * count,
        size=2 * width * part * count,
    )


def weight_gradient(places, flags, slots, turned, so_far, features):
    part, count = slots.part, len(slots.blocks)
    units, rows_all = turned.shape
    tile = min(units, 512)
    tiles = units // tile
    given = len(slots.arrays)
    step = min(part, 1024)
    ahead = min(4, tiles)
    behind = min(4, tiles)

    def body(p_ref, f_ref, *refs):
        h_ref = refs[given]
        w_ref, held, t_sem, turned_held, out_held, h_sem, o_sem = refs[-7:]

        def fetch(i):
            slot = i % ahead
            pltpu.make_async_copy(h_ref.at[block(i, tile)], turned_held.at[slot], h_sem.at[slot]).start()

        def store(i, j):
            columns = pl.ds(pl.multiple_of(p_ref[j] * part, part), part)
            return pltpu.make_async_copy(
                out_held.at[i % behind, j], w_ref.at[block(i, tile), columns], o_sem.at[i % behind, j]
            )

        fetch(0)
        for j in range(count):
            slots.load(j, f_ref, refs[:given], held, t_sem)
        for i in range(1, ahead):
            fetch(i)
        yield

        @pl.loop(0, tiles)
        def _(i):
            wait(turned_held.at[i % ahead], h_sem.at[i % ahead])
            left = turned_held[i % ahead]

            @pl.when(i >= behind)
            def _():
                for j in range(count):
                    store(i - behind, j).wait()

            for j in range(count):

                @pl.when(i == 0)
                def _(j=j):
                    wait(held.at[j], t_sem.at[j])

                for k in range(0, part, step):
                    lanes = pl.ds(k, step)
                    out_held[i % behind, j, :, lanes] = jnp.dot(
                        left, held[j, :, lanes], preferred_element_type=F32
                    ).astype(BF16)
                store(i, j).start()

            @pl.when(i + ahead < tiles)
            def _():
                fetch(i + ahead)

        for i in range(tiles - behind, tiles):
            for j in range(count):
                store(i, j).wait()

    extra = [] if so_far is None else [so_far]
    return dict(
        body=body,
        scalars=2,
        numbers=[places, flags],
        inputs=[*slots.arrays, turned, *extra],
        shapes=[jax.ShapeDtypeStruct((units, features), BF16)],
        aliases={3 + given: 0} if extra else {},
        scratch=slots.scratch()
        + [
            pltpu.VMEM((ahead, tile, rows_all), BF16),
            pltpu.VMEM((behind, count, tile, part), BF16),
            pltpu.SemaphoreType.DMA((ahead,)),
            pltpu.SemaphoreType.DMA((behind, count)),
        ],
        flops=2 * rows_all * units * part * count,
        size=2 * units * part * count,
    )


def tie(values, *deps):
    count = len(values)

    def body(*refs):
        pass

    return pl.pallas_call(
        body,
        in_specs=[ANY] * (count + len(deps)),
        out_specs=[ANY] * count,
        out_shape=[jax.ShapeDtypeStruct(v.shape, v.dtype) for v in values],
        input_output_aliases={i: i for i in range(count)},
        compiler_params=params(),
    )(*values, *deps)


def choose(flags, pairs, values, deps):
    arrays = [piece for pair in pairs for block in pair for piece in block]
    tokens, part = sum(p.shape[0] for p in pairs[0][0]), pairs[0][0][0].shape[1]
    count, kept = len(arrays), len(values)

    def body(f_ref, *refs):
        o_ref, semaphore = refs[-2 - kept], refs[-1]
        given = iter(refs[:count])
        for j, pair in enumerate(pairs):
            for wanted, block in zip((1, 0), pair):
                copies, row = [], j * tokens
                for piece in block:
                    size = piece.shape[0]
                    copies.append(pltpu.make_async_copy(next(given), o_ref.at[pl.ds(row, size)], semaphore))
                    row += size

                @pl.when(f_ref[j] == wanted)
                def _(copies=copies):
                    for copy in copies:
                        copy.start()

        pltpu.make_async_copy(o_ref, o_ref, semaphore).wait()

    return pl.pallas_call(
        body,
        in_specs=[pl.BlockSpec(memory_space=pltpu.SMEM)] + [ANY] * (count + kept + len(deps)),
        out_specs=[ANY] * (1 + kept),
        out_shape=[jax.ShapeDtypeStruct((len(pairs) * tokens, part), BF16)]
        + [jax.ShapeDtypeStruct(v.shape, v.dtype) for v in values],
        input_output_aliases={1 + count + i: 1 + i for i in range(kept)},
        scratch_shapes=[pltpu.SemaphoreType.DMA],
        compiler_params=params(),
    )(flags, *arrays, *values, *deps)


def ring_shards(n, gate_input, up_input, code_values, exponents, cotangent):
    tokens, part = cotangent.shape
    units, features = code_values.shape
    lines = n // 2
    ring = [2 * p for p in range(lines)] + [2 * (n - 1 - p) + 1 for p in range(lines, n)]
    forward = [(ring[p], ring[(p + 1) % n]) for p in range(n)]
    backward = [(b, a) for a, b in forward]
    core = lax.axis_index("depth")
    index = lax.axis_index("grid")
    line = index // 2
    here = jnp.where(index % 2 == 0, line, n - 1 - line)

    def owner(offset):
        p = (here + offset + n) % n
        return jnp.where(p < lines, 2 * p, 2 * (n - 1 - p) + 1)

    def swap(value):
        return lax.ppermute(value, "depth", SWAP)

    def on(value):
        return lax.ppermute(value, "grid", forward)

    def back(value):
        return lax.ppermute(value, "grid", backward)

    pairs = [(4, 0), (3, -1), (-3, 1), (2, -2)]
    mine = [owner(a) // lines == core for a, _ in pairs]
    place = [jnp.where(m, owner(a), owner(b)) % lines for (a, b), m in zip(pairs, mine)]

    def places(*group):
        return jnp.stack([place[j] for j in group]).astype(jnp.int32)

    def flags(*group):
        return jnp.stack([mine[j] for j in group]).astype(jnp.int32)

    half = tokens // 2
    block, got, term = {0: [cotangent]}, {}, {}

    def pieces(rows):
        return [(piece, 0, piece.shape[0]) for piece in rows]

    def terms(*group, deps=()):
        own, others, *turned = output_terms(
            places(*group), hidden, hidden_other, code_values, exponents, part, deps, group == (0,)
        )
        return own, swap(others), *turned

    def keep_terms(group, own, others):
        for i, j in enumerate(group):
            a, b = pairs[j]
            here, there = (rows[i * tokens : (i + 1) * tokens] for rows in (own, others))
            term[a] = jnp.where(mine[j], here, there)
            term[b] = jnp.where(mine[j], there, here)

    def slots(*group):
        return Slots([[pieces(block[a]), pieces(block[b]), got[j]] for j in group for a, b in (pairs[j],)])

    def weight_phase(so_far, group):
        return weight_gradient(places(*group), flags(*group), slots(*group), turned, so_far, features)

    def gradient(so_far, group, deps=()):
        (((out,)),) = run([weight_phase(so_far, group)], deps)
        return out

    def add(value, other):
        return (value.astype(F32) + other.astype(F32)).astype(BF16)

    def exchange(group, values, *deps):
        chosen = [(block[pairs[j][1]], block[pairs[j][0]]) for j in group]
        given, *values = choose(flags(*group), chosen, values, deps)
        found = swap(given)
        for i, j in enumerate(group):
            got[j] = [(found, i * tokens, tokens)]
        return values

    block[-1], block[1] = [on(cotangent)], [back(cotangent)]
    hidden = make_hidden(gate_input, up_input)
    hidden_other = swap(hidden)

    own_a, others_a, turned = terms(0)
    first, second = tie([block[-1][0], block[1][0]], own_a)
    block[-1], block[1] = [first], [second]
    block[-2], block[2] = [on(first)], [back(second)]

    own_b, others_b = terms(1, 2, deps=(first, second))
    first, second = tie([block[-2][0], block[2][0]], own_b)
    block[-2], block[2] = [first], [second]
    block[-3], block[3] = [on(first)], [back(second)]
    exchange((3,), [])

    own_c, others_c = terms(3, deps=(first, second))
    (others_a,) = tie([others_a], own_c)
    keep_terms((0,), own_a, others_a)
    up, down = on(term[4][:half]), back(term[4][half:])
    grad_weight = gradient(None, (3,), (own_c, term[4]))

    first, second, up, down = tie([block[-3][0], block[3][0], up, down], grad_weight)
    block[-3], block[3] = [first], [second]
    block[4] = [on(first[:half]), back(second[half:])]
    exchange((1, 2), [])
    keep_terms((1, 2), own_b, others_b)
    zero = jnp.zeros((half, part), BF16)
    up, down = add(jnp.concatenate([up, zero], 0), term[3]), add(jnp.concatenate([zero, down], 0), term[-3])
    deps = (up, down)
    up, down = on(up), back(down)
    grad_weight = gradient(grad_weight, (1, 2), deps)

    *block[4], up, down = tie([*block[4], up, down], grad_weight)
    exchange((0,), [])
    keep_terms((3,), own_c, others_c)
    up, down = add(up, term[2]), add(down, term[-2])
    deps = (up, down)
    up, down = on(up), back(down)

    everything = slots(0, 1, 2, 3)
    width = units // 2

    def hidden_phase(start, alone):
        return hidden_gradient(
            places(0, 1, 2, 3), flags(0, 1, 2, 3), everything, code_values, exponents, start, width, alone
        )

    (grad_weight,), (own_left, give) = run([weight_phase(grad_weight, (0,)), hidden_phase(0, False)], deps, 36 * 1024 * 1024)
    other_left = swap(give)
    up, down = tie([up, down], give)
    up, down = add(up, term[1]), add(down, term[-1])
    deps = (up, down)
    up, down = on(up), back(down)
    ((own_right, give),) = run([hidden_phase(width, True)], deps)
    other_right = swap(give)
    up, down = tie([up, down], give)
    output_rows = (up.astype(F32) + down.astype(F32) + term[0].astype(F32)).astype(BF16)
    done = finish(gate_input, up_input, own_left, other_left, 0, [], output_rows)
    done = finish(gate_input, up_input, own_right, other_right, width, done)
    return output_rows, done[0], done[1], grad_weight


def any_shards(n, gate_input, up_input, code_values, exponents, cotangent):
    tokens, part = cotangent.shape
    units, features = code_values.shape
    core = lax.axis_index("depth")
    half = n // 2
    gathered = lax.all_gather(cotangent, "grid", axis=0, tiled=False)
    hidden = make_hidden(gate_input, up_input)
    hidden_other = lax.ppermute(hidden, "depth", SWAP)
    place, flag = jnp.zeros((1,), jnp.int32), jnp.ones((1,), jnp.int32)

    own, other, turned = output_terms(
        place, hidden, hidden_other, code_values, exponents, features, turn=True
    )
    got = lax.ppermute(other, "depth", SWAP)
    first = jnp.where(core == 0, own, got).reshape(tokens, half, part)
    second = jnp.where(core == 0, got, own).reshape(tokens, half, part)
    pieces = jnp.concatenate([first, second], 1).transpose(1, 0, 2)
    output_rows = lax.psum_scatter(pieces, "grid", scatter_dimension=0, tiled=False)

    keep = lax.dynamic_slice_in_dim(gathered, core * half, half, 0)
    give = lax.dynamic_slice_in_dim(gathered, (1 - core) * half, half, 0)
    both = [keep, lax.ppermute(give, "depth", SWAP)]
    own, other = ([(v.transpose(1, 0, 2).reshape(tokens, features), 0, tokens)] for v in both)
    slots = Slots([[own, own, other]])
    ((grad_mine, grad_give),) = run([hidden_gradient(place, flag, slots, code_values, exponents, 0, units)])
    grad_other = lax.ppermute(grad_give, "depth", SWAP)
    ((grad_weight,),) = run([weight_gradient(place, flag, slots, turned, None, features)])
    grad_gate, grad_up = finish(gate_input, up_input, grad_mine, grad_other, 0, [])
    return output_rows, grad_gate, grad_up, grad_weight


def solution(mesh):
    n = mesh.shape["grid"]
    in_specs = (
        P(("parts", "depth"), "grid"),
        P(("parts", "depth"), "grid"),
        P("grid", "depth"),
        P("grid", "depth"),
        P(("parts", "depth"), "grid"),
    )
    out_specs = (
        P(("parts", "depth"), "grid"),
        P(("parts", "depth"), "grid"),
        P(("parts", "depth"), "grid"),
        P(("parts", "grid"), "depth"),
    )
    step = functools.partial(ring_shards if n == 8 else any_shards, n)
    return jax.shard_map(step, mesh=mesh, in_specs=in_specs, out_specs=out_specs, check_vma=False)
```

profile of v0, /device:TPU:0, one launch (start us, length us, event | category | flops | bytes accessed | tf_op | source)
XLA Modules:
  0.0 123.4 jit_solution(13393500989257824382)
XLA Ops:
  0.6 3.5 %shard_map.84.h_ref = bf16[256,4096]{1,0:T(8,128)(2,1)} custom-call(bf16[256,4096]{1,0:T(8,128)(2,1)} %g_ref.5, bf16[256,4096]{1,0:T(8,128)(2,1)} %u_ref.5), custom_call_target="tpu_custom_call" | custom-call | flops 10485760 | bytes 6291456 | tf_op jit(solution)/shard_map/pallas_call | solution.py:61
  4.1 0.5 collective-permute-start.2
  4.7 2.6 %collective-permute-start.1 = (bf16[256,1024]{1,0:T(8,128)(2,1)}, bf16[256,1024]{1,0:T(8,128)(2,1)S(1)}, u32[]{:S(2)}, u32[]{:S(2)}) collective-permute-start(bf16[256,1024]{1,0:T(8,128)(2,1)} %refs_4_.3), channel_id=1, source_target_pairs={{4,0},{8,4},{12,8},{14,12},{10,14},{6,10},{2,6},{0,2},{5,1},{9,5},... | collective-permute-start | bytes 1572872 | tf_op jit(solution)/shard_map/ppermute | solution.py:565
  7.2 0.1 collective-permute-start
  7.4 0.1 pad_add_fusion.p_ref.refs_0_
  7.5 0.1 add_convert_fusion.7.f_ref.refs_1_
  7.6 1.2 collective-permute-done.2.x_ref
  8.8 1.6 %copy-done.1 = bf16[256,4096]{1,0:T(8,128)(2,1)S(1)} copy-done((bf16[256,4096]{1,0:T(8,128)(2,1)S(1)}, bf16[256,4096]{1,0:T(8,128)(2,1)}, u32[]{:S(2)}) %copy-start.1) | copy-done | bytes 2097176
  10.4 7.4 %shard_map.85 = (bf16[256,1024]{1,0:T(8,128)(2,1)S(1)}, bf16[256,1024]{1,0:T(8,128)(2,1)S(1)}, bf16[4096,512]{1,0:T(8,128)(2,1)S(1)}) custom-call(s32[1]{0:T(128)} %bitcast.p_ref.refs_0_, bf16[256,4096]{1,0:T(8,128)(2,1)S(1)} %copy-done.1, bf16[256,4096]{1,0:T(8,128)(2,1)} %collective-permute-done.2.x_ref, bf16[4096,4096]{1,0:T(8,128)(2,1)} %refs_15_.1, ...), custom_call_target="tpu_custom_call" | custom-call | flops 4294967296 | bytes 8388608 | tf_op jit(solution)/shard_map/pallas_call | solution.py:200
  17.8 2.2 %collective-permute-done.1.refs_1_ = bf16[256,1024]{1,0:T(8,128)(2,1)S(1)} collective-permute-done((bf16[256,1024]{1,0:T(8,128)(2,1)}, bf16[256,1024]{1,0:T(8,128)(2,1)S(1)}, u32[]{:S(2)}, u32[]{:S(2)}) %collective-permute-start.1) | collective-permute-done | bytes 524320 | tf_op jit(solution)/shard_map/ppermute | solution.py:565
  20.0 1.4 %collective-permute-done.refs_0_ = bf16[256,1024]{1,0:T(8,128)(2,1)S(1)} collective-permute-done((bf16[256,1024]{1,0:T(8,128)(2,1)}, bf16[256,1024]{1,0:T(8,128)(2,1)S(1)}, u32[]{:S(2)}, u32[]{:S(2)}) %collective-permute-start) | collective-permute-done | bytes 524320 | tf_op jit(solution)/shard_map/ppermute | solution.py:562
  21.4 0.4 collective-permute-start.3
  21.8 1.7 %collective-permute-start.4 = (bf16[256,1024]{1,0:T(8,128)(2,1)S(1)}, bf16[256,1024]{1,0:T(8,128)(2,1)S(1)}, u32[]{:S(2)}, u32[]{:S(2)}) collective-permute-start(bf16[256,1024]{1,0:T(8,128)(2,1)S(1)} %get-tuple-element.38.refs_1_.refs_2_.refs_6_.refs_18_.refs_10_), channel_id=1, source_target_pairs={{4,0},{8,4},{12,8},{14,12},{10,14},{6,10},{2,6},{0,2},{5,1},{9,5},... | collective-permute-start | bytes 1572872 | tf_op jit(solution)/shard_map/ppermute | solution.py:565
  23.5 12.6 %shard_map.87 = (bf16[512,1024]{1,0:T(8,128)(2,1)S(1)}, bf16[512,1024]{1,0:T(8,128)(2,1)S(1)}) custom-call(s32[2]{0:T(128)S(1)} %pad_add_fusion.p_ref.refs_0_, bf16[256,4096]{1,0:T(8,128)(2,1)S(1)} %copy-done.1, bf16[256,4096]{1,0:T(8,128)(2,1)} %collective-permute-done.2.x_ref, bf16[4096,4096]{1,0:T(8,128)(2,1)} %refs_15_.1, s32[128,4096]{1,0:T(8,128)S(1)} %copy-done, ...), custom_call_target="tpu_custom_call" | custom-call | flops 8589934592 | bytes 16777216 | tf_op jit(solution)/shard_map/pallas_call | solution.py:200
  36.1 0.6 collective-permute-start.13
  36.7 0.4 collective-permute-start.5
  37.0 1.7 %collective-permute-start.6 = (bf16[256,1024]{1,0:T(8,128)(2,1)S(1)}, bf16[256,1024]{1,0:T(8,128)(2,1)S(1)}, u32[]{:S(2)}, u32[]{:S(2)}) collective-permute-start(bf16[256,1024]{1,0:T(8,128)(2,1)S(1)} %get-tuple-element.41.refs_1_.refs_2_.refs_20_.refs_12_), channel_id=1, source_target_pairs={{4,0},{8,4},{12,8},{14,12},{10,14},{6,10},{2,6},{0,2},{5,1},{9,5},... | collective-permute-start | bytes 1572872 | tf_op jit(solution)/shard_map/ppermute | solution.py:565
  38.7 0.2 shard_map.91
  38.9 0.1 collective-permute-start.10
  39.0 7.1 %shard_map.89 = (bf16[256,1024]{1,0:T(8,128)(2,1)S(1)}, bf16[256,1024]{1,0:T(8,128)(2,1)S(1)}) custom-call(s32[1]{0:T(128)} %bitcast.3.p_ref.refs_0_, bf16[256,4096]{1,0:T(8,128)(2,1)S(1)} %copy-done.1, bf16[256,4096]{1,0:T(8,128)(2,1)} %collective-permute-done.2.x_ref, bf16[4096,4096]{1,0:T(8,128)(2,1)} %refs_15_.1, s32[128,4096]{1,0:T(8,128)S(1)} %copy-done, ...), custom_call_target="tpu_custom_call" | custom-call | flops 4294967296 | bytes 8388608 | tf_op jit(solution)/shard_map/pallas_call | solution.py:200
  46.1 0.0 collective-permute-done.7.refs_0_
  46.1 0.1 broadcast_select_fusion.refs_7_
  46.2 1.6 %collective-permute-start.9 = (bf16[128,1024]{1,0:T(8,128)(2,1)S(1)}, bf16[128,1024]{1,0:T(8,128)(2,1)S(1)}, u32[]{:S(2)}, u32[]{:S(2)}) collective-permute-start(bf16[128,1024]{1,0:T(8,128)(2,1)S(1)} %get-tuple-element.74), channel_id=1, source_target_pairs={{4,0},{8,4},{12,8},{14,12},{10,14},{6,10},{2,6},{0,2},{5,1},{9,5},... | collective-permute-start | bytes 786440 | tf_op jit(solution)/shard_map/ppermute | solution.py:565
  47.9 0.0 collective-permute-done.10.refs_4_.refs_22_.refs_14_
  47.9 0.4 collective-permute-start.8
  48.3 7.5 %shard_map.92.refs_4_.refs_9_ = bf16[4096,4096]{1,0:T(8,128)(2,1)} custom-call(s32[1]{0:T(128)} %bitcast.3.p_ref.refs_0_, s32[1]{0:T(128)S(6)} %convert_element_type.82.f_ref.refs_1_, bf16[256,1024]{1,0:T(8,128)(2,1)S(1)} %get-tuple-element.41.refs_1_.refs_2_.refs_20_.refs_12_, bf16[256,1024]{1,0:T(8,128)(2,1)S(1)} %get-tuple-element.40.refs_0_.refs_3_.refs_21_.refs_13_, ...), custom_call_target="tpu_custom_call" | custom-call | flops 4294967296 | bytes 8388608 | tf_op jit(solution)/shard_map/pallas_call | solution.py:284
  55.8 0.5 collective-permute-done.9.refs_3_
  56.3 0.0 collective-permute-done.8.refs_2_
  56.3 0.0 collective-permute-done.5.refs_0_
  56.3 0.7 shard_map.94
  57.0 0.1 collective-permute-start.16
  57.1 0.5 collective-permute-start.17
  57.6 1.7 %collective-permute-start.12 = (bf16[128,1024]{1,0:T(8,128)(2,1)S(1)}, bf16[128,1024]{1,0:T(8,128)(2,1)S(1)}, u32[]{:S(2)}, u32[]{:S(2)}) collective-permute-start(bf16[128,1024]{1,0:T(8,128)(2,1)S(1)} %slice.27), channel_id=1, source_target_pairs={{4,0},{8,4},{12,8},{14,12},{10,14},{6,10},{2,6},{0,2},{5,1},{9,5},... | collective-permute-start | bytes 786440 | tf_op jit(solution)/shard_map/ppermute | solution.py:565
  59.3 0.4 collective-permute-start.11
  59.7 0.5 add_convert_fusion.5
  60.2 1.7 %collective-permute-start.15 = (bf16[256,1024]{1,0:T(8,128)(2,1)S(1)}, bf16[256,1024]{1,0:T(8,128)(2,1)S(1)}, u32[]{:S(2)}, u32[]{:S(2)}) collective-permute-start(bf16[256,1024]{1,0:T(8,128)(2,1)S(1)} %get-tuple-element.70.refs_11_), channel_id=1, source_target_pairs={{4,0},{8,4},{12,8},{14,12},{10,14},{6,10},{2,6},{0,2},{5,1},{9,5},... | collective-permute-start | bytes 1572872 | tf_op jit(solution)/shard_map/ppermute | solution.py:565
  61.9 0.4 collective-permute-start.14
  62.3 13.9 %shard_map.95.refs_4_.refs_7_ = bf16[4096,4096]{1,0:T(8,128)(2,1)} custom-call(s32[2]{0:T(128)S(1)} %pad_add_fusion.p_ref.refs_0_, s32[2]{0:T(128)S(1)} %add_convert_fusion.7.f_ref.refs_1_, bf16[256,1024]{1,0:T(8,128)(2,1)S(1)} %get-tuple-element.46.refs_1_.refs_2_.refs_14_.refs_6_, ...), custom_call_target="tpu_custom_call", output_to_operand_aliasing={{}: (9, {})} | custom-call | flops 8589934592 | bytes 16777216 | tf_op jit(solution)/shard_map/pallas_call | solution.py:284
  76.2 0.0 collective-permute-done.12.refs_1_
  76.2 1.0 collective-permute-done.15.refs_3_
  77.2 1.4 %collective-permute-done.14.refs_2_ = bf16[256,1024]{1,0:T(8,128)(2,1)S(1)} collective-permute-done((bf16[256,1024]{1,0:T(8,128)(2,1)S(1)}, bf16[256,1024]{1,0:T(8,128)(2,1)S(1)}, u32[]{:S(2)}, u32[]{:S(2)}) %collective-permute-start.14) | collective-permute-done | bytes 524320 | tf_op jit(solution)/shard_map/ppermute | solution.py:562
  78.6 0.1 collective-permute-start.20
  78.7 0.1 pad_add_fusion.1.refs_8_.refs_0_
  78.8 0.1 add_convert_fusion.8.refs_9_.refs_1_
  78.9 0.4 add_convert_fusion.3
  79.3 1.6 %collective-permute-start.19 = (bf16[256,1024]{1,0:T(8,128)(2,1)S(1)}, bf16[256,1024]{1,0:T(8,128)(2,1)S(1)}, u32[]{:S(2)}, u32[]{:S(2)}) collective-permute-start(bf16[256,1024]{1,0:T(8,128)(2,1)S(1)} %get-tuple-element.72.refs_26_), channel_id=1, source_target_pairs={{4,0},{8,4},{12,8},{14,12},{10,14},{6,10},{2,6},{0,2},{5,1},{9,5},... | collective-permute-start | bytes 1572872 | tf_op jit(solution)/shard_map/ppermute | solution.py:565
  81.0 0.4 collective-permute-start.18
  81.4 0.0 collective-permute-done.20.refs_5_.refs_13_
  81.4 19.2 %shard_map.98 = (bf16[4096,4096]{1,0:T(8,128)(2,1)}, f32[256,2048]{1,0:T(8,128)S(1)}, bf16[256,2048]{1,0:T(8,128)(2,1)S(1)}) custom-call(s32[1]{0:T(128)} %bitcast.p_ref.refs_0_, s32[1]{0:T(128)S(6)} %convert_element_type.96.f_ref.refs_1_, bf16[128,1024]{1,0:T(8,128)(2,1)S(1)} %get-tuple-element.53.refs_1_.refs_2_.refs_10_, ...), custom_call_target="tpu_custom_call", output_to_operand_aliasing={{0}: (7, {})} | custom-call | flops 12884901888 | bytes 25165824 | tf_op jit(solution)/shard_map/pallas_call | solution.py:284
  100.6 0.1 collective-permute-start.24
  100.7 0.6 add_convert_fusion.1
  101.3 1.6 %collective-permute-start.22 = (bf16[256,1024]{1,0:T(8,128)(2,1)S(1)}, bf16[256,1024]{1,0:T(8,128)(2,1)S(1)}, u32[]{:S(2)}, u32[]{:S(2)}) collective-permute-start(bf16[256,1024]{1,0:T(8,128)(2,1)S(1)} %get-tuple-element.68.refs_18_), channel_id=1, source_target_pairs={{4,0},{8,4},{12,8},{14,12},{10,14},{6,10},{2,6},{0,2},{5,1},{9,5},... | collective-permute-start | bytes 1572872 | tf_op jit(solution)/shard_map/ppermute | solution.py:565
  103.0 0.4 collective-permute-start.21
  103.4 12.8 %shard_map.100 = (f32[256,2048]{1,0:T(8,128)S(1)}, bf16[256,2048]{1,0:T(8,128)(2,1)S(1)}) custom-call(s32[4]{0:T(128)S(1)} %pad_add_fusion.1.refs_8_.refs_0_, s32[4]{0:T(128)S(1)} %add_convert_fusion.8.refs_9_.refs_1_, bf16[128,1024]{1,0:T(8,128)(2,1)S(1)} %get-tuple-element.53.refs_1_.refs_2_.refs_10_, ...), custom_call_target="tpu_custom_call" | custom-call | flops 8589934592 | bytes 16777216 | tf_op jit(solution)/shard_map/pallas_call | solution.py:284
  116.2 0.0 copy-start.2
  116.2 0.0 copy-start.3
  116.2 0.1 collective-permute-start.23
  116.3 1.0 collective-permute-done.21.refs_0_
  117.4 0.4 add_convert_fusion.refs_0_
  117.7 0.0 copy-start.4
  117.8 0.0 copy-done.2
  117.8 0.6 copy-done.3
  118.4 2.5 %shard_map.102 = (bf16[256,4096]{1,0:T(8,128)(2,1)}, bf16[256,4096]{1,0:T(8,128)(2,1)}) custom-call(bf16[256,4096]{1,0:T(8,128)(2,1)S(1)} %copy-done.2, bf16[256,4096]{1,0:T(8,128)(2,1)S(1)} %copy-done.3, f32[256,2048]{1,0:T(8,128)S(1)} %get-tuple-element.62.m_ref, bf16[256,2048]{1,0:T(8,128)(2,1)S(1)} %collective-permute-done.24.o_ref, ...), custom_call_target="tpu_custom_call" | custom-call | flops 10485760000 | bytes 524288000 | tf_op jit(solution)/shard_map/pallas_call | solution.py:90
  120.9 2.5 %shard_map.103 = (bf16[256,4096]{1,0:T(8,128)(2,1)}, bf16[256,4096]{1,0:T(8,128)(2,1)}) custom-call(bf16[256,4096]{1,0:T(8,128)(2,1)S(1)} %copy-done.2, bf16[256,4096]{1,0:T(8,128)(2,1)S(1)} %copy-done.3, f32[256,2048]{1,0:T(8,128)S(1)} %get-tuple-element.61.m_ref, ...), custom_call_target="tpu_custom_call", output_to_operand_aliasing={{0}: (4, {}), {1}: (5, {})} | custom-call | flops 10485760000 | bytes 524288000 | tf_op jit(solution)/shard_map/pallas_call | solution.py:90
  (28 shorter events, 0.2 us)
Async XLA Ops:
  0.6 8.2 %copy-start = (s32[128,4096]{1,0:T(8,128)S(1)}, s32[128,4096]{1,0:T(8,128)}, u32[]{:S(2)}) copy-start(s32[128,4096]{1,0:T(8,128)} %refs_16_.1) | copy-start | bytes 6291460
  4.1 4.6 %collective-permute-start.2 = (bf16[256,4096]{1,0:T(8,128)(2,1)}, bf16[256,4096]{1,0:T(8,128)(2,1)}, u32[]{:S(2)}, u32[]{:S(2)}) collective-permute-start(bf16[256,4096]{1,0:T(8,128)(2,1)} %shard_map.84.h_ref), channel_id=1, source_target_pairs={{0,1},{1,0},{2,3},{3,2},{4,5},{5,4},{6,7},{7,6},{8,9},{9,8},{10,11... | collective-permute-start | bytes 6291464 | tf_op jit(solution)/shard_map/ppermute | solution.py:559
  4.7 15.4 %collective-permute-start.1 = (bf16[256,1024]{1,0:T(8,128)(2,1)}, bf16[256,1024]{1,0:T(8,128)(2,1)S(1)}, u32[]{:S(2)}, u32[]{:S(2)}) collective-permute-start(bf16[256,1024]{1,0:T(8,128)(2,1)} %refs_4_.3), channel_id=1, source_target_pairs={{4,0},{8,4},{12,8},{14,12},{10,14},{6,10},{2,6},{0,2},{5,1},{9,5},... | collective-permute-start | bytes 1572872 | tf_op jit(solution)/shard_map/ppermute | solution.py:565
  7.2 14.2 %collective-permute-start = (bf16[256,1024]{1,0:T(8,128)(2,1)}, bf16[256,1024]{1,0:T(8,128)(2,1)S(1)}, u32[]{:S(2)}, u32[]{:S(2)}) collective-permute-start(bf16[256,1024]{1,0:T(8,128)(2,1)} %refs_4_.3), channel_id=1, source_target_pairs={{0,4},{4,8},{8,12},{12,14},{14,10},{10,6},{6,2},{2,0},{1,5},{5,9},... | collective-permute-start | bytes 1572872 | tf_op jit(solution)/shard_map/ppermute | solution.py:562
  8.8 1.6 %copy-start.1 = (bf16[256,4096]{1,0:T(8,128)(2,1)S(1)}, bf16[256,4096]{1,0:T(8,128)(2,1)}, u32[]{:S(2)}) copy-start(bf16[256,4096]{1,0:T(8,128)(2,1)} %shard_map.84.h_ref) | copy-start | bytes 6291460
  21.4 15.2 %collective-permute-start.3 = (bf16[256,1024]{1,0:T(8,128)(2,1)S(1)}, bf16[256,1024]{1,0:T(8,128)(2,1)S(1)}, u32[]{:S(2)}, u32[]{:S(2)}) collective-permute-start(bf16[256,1024]{1,0:T(8,128)(2,1)S(1)} %get-tuple-element.37.refs_0_.refs_3_.refs_15_.refs_7_), channel_id=1, source_target_pairs={{0,4},{4,8},{8,12},{12,14},{14,10},{10,6},{6,2},{2,0},{1,5},{5,9},... | collective-permute-start | bytes 1572872 | tf_op jit(solution)/shard_map/ppermute | solution.py:562
  21.8 14.9 %collective-permute-start.4 = (bf16[256,1024]{1,0:T(8,128)(2,1)S(1)}, bf16[256,1024]{1,0:T(8,128)(2,1)S(1)}, u32[]{:S(2)}, u32[]{:S(2)}) collective-permute-start(bf16[256,1024]{1,0:T(8,128)(2,1)S(1)} %get-tuple-element.38.refs_1_.refs_2_.refs_6_.refs_18_.refs_10_), channel_id=1, source_target_pairs={{4,0},{8,4},{12,8},{14,12},{10,14},{6,10},{2,6},{0,2},{5,1},{9,5},... | collective-permute-start | bytes 1572872 | tf_op jit(solution)/shard_map/ppermute | solution.py:565
  23.5 22.6 %collective-permute-start.7 = (bf16[256,1024]{1,0:T(8,128)(2,1)S(1)}, bf16[256,1024]{1,0:T(8,128)(2,1)S(1)}, u32[]{:S(2)}, u32[]{:S(2)}) collective-permute-start(bf16[256,1024]{1,0:T(8,128)(2,1)S(1)} %get-tuple-element.42), channel_id=1, source_target_pairs={{0,1},{1,0},{2,3},{3,2},{4,5},{5,4},{6,7},{7,6},{8,9},{9,8},{10,11... | collective-permute-start | bytes 1572872 | tf_op jit(solution)/shard_map/ppermute | solution.py:559
  36.1 23.6 %collective-permute-start.13 = (bf16[512,1024]{1,0:T(8,128)(2,1)S(1)}, bf16[512,1024]{1,0:T(8,128)(2,1)S(1)}, u32[]{:S(2)}, u32[]{:S(2)}) collective-permute-start(bf16[512,1024]{1,0:T(8,128)(2,1)S(1)} %get-tuple-element.48), channel_id=1, source_target_pairs={{0,1},{1,0},{2,3},{3,2},{4,5},{5,4},{6,7},{7,6},{8,9},{9,8},{10,11... | collective-permute-start | bytes 3145736 | tf_op jit(solution)/shard_map/ppermute | solution.py:559
  36.7 19.6 %collective-permute-start.5 = (bf16[256,1024]{1,0:T(8,128)(2,1)S(1)}, bf16[256,1024]{1,0:T(8,128)(2,1)S(1)}, u32[]{:S(2)}, u32[]{:S(2)}) collective-permute-start(bf16[256,1024]{1,0:T(8,128)(2,1)S(1)} %get-tuple-element.40.refs_0_.refs_3_.refs_21_.refs_13_), channel_id=1, source_target_pairs={{0,4},{4,8},{8,12},{12,14},{14,10},{10,6},{6,2},{2,0},{1,5},{5,9},... | collective-permute-start | bytes 1572872 | tf_op jit(solution)/shard_map/ppermute | solution.py:562
  37.0 19.3 %collective-permute-start.6 = (bf16[256,1024]{1,0:T(8,128)(2,1)S(1)}, bf16[256,1024]{1,0:T(8,128)(2,1)S(1)}, u32[]{:S(2)}, u32[]{:S(2)}) collective-permute-start(bf16[256,1024]{1,0:T(8,128)(2,1)S(1)} %get-tuple-element.41.refs_1_.refs_2_.refs_20_.refs_12_), channel_id=1, source_target_pairs={{4,0},{8,4},{12,8},{14,12},{10,14},{6,10},{2,6},{0,2},{5,1},{9,5},... | collective-permute-start | bytes 1572872 | tf_op jit(solution)/shard_map/ppermute | solution.py:565
  38.9 8.9 %collective-permute-start.10 = (bf16[256,1024]{1,0:T(8,128)(2,1)S(1)}, bf16[256,1024]{1,0:T(8,128)(2,1)S(1)}, u32[]{:S(2)}, u32[]{:S(2)}) collective-permute-start(bf16[256,1024]{1,0:T(8,128)(2,1)S(1)} %shard_map.91), channel_id=1, source_target_pairs={{0,1},{1,0},{2,3},{3,2},{4,5},{5,4},{6,7},{7,6},{8,9},{9,8},{10,11... | collective-permute-start | bytes 1572872 | tf_op jit(solution)/shard_map/ppermute | solution.py:559
  46.2 10.1 %collective-permute-start.9 = (bf16[128,1024]{1,0:T(8,128)(2,1)S(1)}, bf16[128,1024]{1,0:T(8,128)(2,1)S(1)}, u32[]{:S(2)}, u32[]{:S(2)}) collective-permute-start(bf16[128,1024]{1,0:T(8,128)(2,1)S(1)} %get-tuple-element.74), channel_id=1, source_target_pairs={{4,0},{8,4},{12,8},{14,12},{10,14},{6,10},{2,6},{0,2},{5,1},{9,5},... | collective-permute-start | bytes 786440 | tf_op jit(solution)/shard_map/ppermute | solution.py:565
  47.9 8.4 %collective-permute-start.8 = (bf16[128,1024]{1,0:T(8,128)(2,1)S(1)}, bf16[128,1024]{1,0:T(8,128)(2,1)S(1)}, u32[]{:S(2)}, u32[]{:S(2)}) collective-permute-start(bf16[128,1024]{1,0:T(8,128)(2,1)S(1)} %get-tuple-element.75), channel_id=1, source_target_pairs={{0,4},{4,8},{8,12},{12,14},{14,10},{10,6},{6,2},{2,0},{1,5},{5,9},... | collective-permute-start | bytes 786440 | tf_op jit(solution)/shard_map/ppermute | solution.py:562
  57.0 4.9 %collective-permute-start.16 = (bf16[512,1024]{1,0:T(8,128)(2,1)S(1)}, bf16[512,1024]{1,0:T(8,128)(2,1)S(1)}, u32[]{:S(2)}, u32[]{:S(2)}) collective-permute-start(bf16[512,1024]{1,0:T(8,128)(2,1)S(1)} %shard_map.94), channel_id=1, source_target_pairs={{0,1},{1,0},{2,3},{3,2},{4,5},{5,4},{6,7},{7,6},{8,9},{9,8},{10,11... | collective-permute-start | bytes 3145736 | tf_op jit(solution)/shard_map/ppermute | solution.py:559
  57.1 21.8 %collective-permute-start.17 = (bf16[256,1024]{1,0:T(8,128)(2,1)S(1)}, bf16[256,1024]{1,0:T(8,128)(2,1)S(1)}, u32[]{:S(2)}, u32[]{:S(2)}) collective-permute-start(bf16[256,1024]{1,0:T(8,128)(2,1)S(1)} %get-tuple-element.51), channel_id=1, source_target_pairs={{0,1},{1,0},{2,3},{3,2},{4,5},{5,4},{6,7},{7,6},{8,9},{9,8},{10,11... | collective-permute-start | bytes 1572872 | tf_op jit(solution)/shard_map/ppermute | solution.py:559
  57.6 18.5 %collective-permute-start.12 = (bf16[128,1024]{1,0:T(8,128)(2,1)S(1)}, bf16[128,1024]{1,0:T(8,128)(2,1)S(1)}, u32[]{:S(2)}, u32[]{:S(2)}) collective-permute-start(bf16[128,1024]{1,0:T(8,128)(2,1)S(1)} %slice.27), channel_id=1, source_target_pairs={{4,0},{8,4},{12,8},{14,12},{10,14},{6,10},{2,6},{0,2},{5,1},{9,5},... | collective-permute-start | bytes 786440 | tf_op jit(solution)/shard_map/ppermute | solution.py:565
  59.3 16.8 %collective-permute-start.11 = (bf16[128,1024]{1,0:T(8,128)(2,1)S(1)}, bf16[128,1024]{1,0:T(8,128)(2,1)S(1)}, u32[]{:S(2)}, u32[]{:S(2)}) collective-permute-start(bf16[128,1024]{1,0:T(8,128)(2,1)S(1)} %slice.26), channel_id=1, source_target_pairs={{0,4},{4,8},{8,12},{12,14},{14,10},{10,6},{6,2},{2,0},{1,5},{5,9},... | collective-permute-start | bytes 786440 | tf_op jit(solution)/shard_map/ppermute | solution.py:562
  60.2 17.0 %collective-permute-start.15 = (bf16[256,1024]{1,0:T(8,128)(2,1)S(1)}, bf16[256,1024]{1,0:T(8,128)(2,1)S(1)}, u32[]{:S(2)}, u32[]{:S(2)}) collective-permute-start(bf16[256,1024]{1,0:T(8,128)(2,1)S(1)} %get-tuple-element.70.refs_11_), channel_id=1, source_target_pairs={{4,0},{8,4},{12,8},{14,12},{10,14},{6,10},{2,6},{0,2},{5,1},{9,5},... | collective-permute-start | bytes 1572872 | tf_op jit(solution)/shard_map/ppermute | solution.py:565
  61.9 16.7 %collective-permute-start.14 = (bf16[256,1024]{1,0:T(8,128)(2,1)S(1)}, bf16[256,1024]{1,0:T(8,128)(2,1)S(1)}, u32[]{:S(2)}, u32[]{:S(2)}) collective-permute-start(bf16[256,1024]{1,0:T(8,128)(2,1)S(1)} %get-tuple-element.71.refs_10_), channel_id=1, source_target_pairs={{0,4},{4,8},{8,12},{12,14},{14,10},{10,6},{6,2},{2,0},{1,5},{5,9},... | collective-permute-start | bytes 1572872 | tf_op jit(solution)/shard_map/ppermute | solution.py:562
  78.6 2.8 %collective-permute-start.20 = (bf16[256,1024]{1,0:T(8,128)(2,1)S(1)}, bf16[256,1024]{1,0:T(8,128)(2,1)S(1)}, u32[]{:S(2)}, u32[]{:S(2)}) collective-permute-start(bf16[256,1024]{1,0:T(8,128)(2,1)S(1)} %shard_map.97), channel_id=1, source_target_pairs={{0,1},{1,0},{2,3},{3,2},{4,5},{5,4},{6,7},{7,6},{8,9},{9,8},{10,11... | collective-permute-start | bytes 1572872 | tf_op jit(solution)/shard_map/ppermute | solution.py:559
  79.3 21.3 %collective-permute-start.19 = (bf16[256,1024]{1,0:T(8,128)(2,1)S(1)}, bf16[256,1024]{1,0:T(8,128)(2,1)S(1)}, u32[]{:S(2)}, u32[]{:S(2)}) collective-permute-start(bf16[256,1024]{1,0:T(8,128)(2,1)S(1)} %get-tuple-element.72.refs_26_), channel_id=1, source_target_pairs={{4,0},{8,4},{12,8},{14,12},{10,14},{6,10},{2,6},{0,2},{5,1},{9,5},... | collective-permute-start | bytes 1572872 | tf_op jit(solution)/shard_map/ppermute | solution.py:565
  81.0 19.7 %collective-permute-start.18 = (bf16[256,1024]{1,0:T(8,128)(2,1)S(1)}, bf16[256,1024]{1,0:T(8,128)(2,1)S(1)}, u32[]{:S(2)}, u32[]{:S(2)}) collective-permute-start(bf16[256,1024]{1,0:T(8,128)(2,1)S(1)} %get-tuple-element.73.refs_25_), channel_id=1, source_target_pairs={{0,4},{4,8},{8,12},{12,14},{14,10},{10,6},{6,2},{2,0},{1,5},{5,9},... | collective-permute-start | bytes 1572872 | tf_op jit(solution)/shard_map/ppermute | solution.py:562
  100.6 17.2 %collective-permute-start.24 = (bf16[256,2048]{1,0:T(8,128)(2,1)S(1)}, bf16[256,2048]{1,0:T(8,128)(2,1)S(1)}, u32[]{:S(2)}, u32[]{:S(2)}) collective-permute-start(bf16[256,2048]{1,0:T(8,128)(2,1)S(1)} %get-tuple-element.55.refs_2_), channel_id=1, source_target_pairs={{0,1},{1,0},{2,3},{3,2},{4,5},{5,4},{6,7},{7,6},{8,9},{9,8},{10,11... | collective-permute-start | bytes 3145736 | tf_op jit(solution)/shard_map/ppermute | solution.py:559
  101.3 15.0 %collective-permute-start.22 = (bf16[256,1024]{1,0:T(8,128)(2,1)S(1)}, bf16[256,1024]{1,0:T(8,128)(2,1)S(1)}, u32[]{:S(2)}, u32[]{:S(2)}) collective-permute-start(bf16[256,1024]{1,0:T(8,128)(2,1)S(1)} %get-tuple-element.68.refs_18_), channel_id=1, source_target_pairs={{4,0},{8,4},{12,8},{14,12},{10,14},{6,10},{2,6},{0,2},{5,1},{9,5},... | collective-permute-start | bytes 1572872 | tf_op jit(solution)/shard_map/ppermute | solution.py:565
  103.0 14.4 %collective-permute-start.21 = (bf16[256,1024]{1,0:T(8,128)(2,1)S(1)}, bf16[256,1024]{1,0:T(8,128)(2,1)S(1)}, u32[]{:S(2)}, u32[]{:S(2)}) collective-permute-start(bf16[256,1024]{1,0:T(8,128)(2,1)S(1)} %get-tuple-element.69.refs_17_), channel_id=1, source_target_pairs={{0,4},{4,8},{8,12},{12,14},{14,10},{10,6},{6,2},{2,0},{1,5},{5,9},... | collective-permute-start | bytes 1572872 | tf_op jit(solution)/shard_map/ppermute | solution.py:562
  116.2 1.6 %copy-start.2 = (bf16[256,4096]{1,0:T(8,128)(2,1)S(1)}, bf16[256,4096]{1,0:T(8,128)(2,1)}, u32[]{:S(2)}) copy-start(bf16[256,4096]{1,0:T(8,128)(2,1)} %g_ref.5) | copy-start | bytes 6291460
  116.2 2.2 %copy-start.3 = (bf16[256,4096]{1,0:T(8,128)(2,1)S(1)}, bf16[256,4096]{1,0:T(8,128)(2,1)}, u32[]{:S(2)}) copy-start(bf16[256,4096]{1,0:T(8,128)(2,1)} %u_ref.5) | copy-start | bytes 6291460
  116.2 4.7 %collective-permute-start.23 = (bf16[256,2048]{1,0:T(8,128)(2,1)S(1)}, bf16[256,2048]{1,0:T(8,128)(2,1)S(1)}, u32[]{:S(2)}, u32[]{:S(2)}) collective-permute-start(bf16[256,2048]{1,0:T(8,128)(2,1)S(1)} %get-tuple-element.58.refs_2_), channel_id=1, source_target_pairs={{0,1},{1,0},{2,3},{3,2},{4,5},{5,4},{6,7},{7,6},{8,9},{9,8},{10,11... | collective-permute-start | bytes 3145736 | tf_op jit(solution)/shard_map/ppermute | solution.py:559
  117.7 3.2 %copy-start.4 = (bf16[256,1024]{1,0:T(8,128)(2,1)}, bf16[256,1024]{1,0:T(8,128)(2,1)S(1)}, u32[]{:S(2)}) copy-start(bf16[256,1024]{1,0:T(8,128)(2,1)S(1)} %add_convert_fusion.refs_0_) | copy-start | bytes 1572868
where the time goes:
time: 124 us; the launch traced here: 123 us
  Pallas kernels  89.8 us (72%)
  starting transfers between devices  19.1 us (15%)
  waiting for transfers between devices  8.86 us (7%)
  local copies, waits for them, and re-layouts  2.36 us (2%)
  other arithmetic  2.31 us (2%)
    pallas_call x4, Pallas kernels, run(): pl.pallas_call(body, in_specs=[spec for p in phases for spec in [smem] *...  53.3 us
    pallas_call x3, Pallas kernels, output_terms(): pl.pallas_call(body, in_specs=[pl.BlockSpec(memory_space=pltpu.SMEM)] + [...  27.1 us
    ppermute x8, starting transfers between devices, back(): return lax.ppermute(value, 'grid', backward)  14.3 us
    pallas_call x2, Pallas kernels, finish(): pl.pallas_call(body, grid=(width // tile,), in_specs=[there, there, here,...  4.97 us
    ppermute x8, waiting for transfers between devices, on(): return lax.ppermute(value, 'grid', forward)  3.85 us
    ppermute x8, waiting for transfers between devices, back(): return lax.ppermute(value, 'grid', backward)  3.8 us
    pallas_call x1, Pallas kernels, make_hidden(): pl.pallas_call(body, in_specs=[ANY] * 2, out_specs=ANY, out_shape=jax.Sha...  3.5 us
    ppermute x8, starting transfers between devices, on(): return lax.ppermute(value, 'grid', forward)  2.9 us
  transfers between devices with their start and end apart: 25, of which 7 were waited for; matrix products, arithmetic and copies ran while one was open for 2% of the time, Pallas kernels for 68%

commit v1 on v0

--- a/solution.py
+++ b/solution.py
@@ -669,10 +669,9 @@
     up, down = on(up), back(down)
     ((own_right, give),) = run([hidden_phase(width, True)], deps)
     other_right = swap(give)
-    up, down = tie([up, down], give)
+    done = finish(gate_input, up_input, own_left, other_left, 0, [], give)
     output_rows = (up.astype(F32) + down.astype(F32) + term[0].astype(F32)).astype(BF16)
-    done = finish(gate_input, up_input, own_left, other_left, 0, [], output_rows)
-    done = finish(gate_input, up_input, own_right, other_right, width, done)
+    done = finish(gate_input, up_input, own_right, other_right, width, done, output_rows)
     return output_rows, done[0], done[1], grad_weight
 
 

time: 124 us -> 123 us (level)
  no operation moved by 1% of the time
where the time goes in v1:
time: 123 us
  Pallas kernels  89.8 us (73%)
  starting transfers between devices  19.1 us (16%)
  waiting for transfers between devices  8.05 us (7%)
  local copies, waits for them, and re-layouts  2.53 us (2%)
  other arithmetic  2.32 us (2%)
    pallas_call x4, Pallas kernels, run(): pl.pallas_call(body, in_specs=[spec for p in phases for spec in [smem] *...  53.3 us
    pallas_call x3, Pallas kernels, output_terms(): pl.pallas_call(body, in_specs=[pl.BlockSpec(memory_space=pltpu.SMEM)] + [...  27.1 us
    ppermute x8, starting transfers between devices, back(): return lax.ppermute(value, 'grid', backward)  13.5 us
    pallas_call x2, Pallas kernels, finish(): pl.pallas_call(body, grid=(width // tile,), in_specs=[there, there, here,...  4.97 us
    ppermute x8, waiting for transfers between devices, back(): return lax.ppermute(value, 'grid', backward)  4.03 us
    ppermute x8, starting transfers between devices, on(): return lax.ppermute(value, 'grid', forward)  3.64 us
    pallas_call x1, Pallas kernels, make_hidden(): pl.pallas_call(body, in_specs=[ANY] * 2, out_specs=ANY, out_shape=jax.Sha...  3.5 us
    ppermute x8, waiting for transfers between devices, on(): return lax.ppermute(value, 'grid', forward)  2.81 us
  transfers between devices with their start and end apart: 25, of which 7 were waited for; matrix products, arithmetic and copies ran while one was open for 2% of the time, Pallas kernels for 68%

profile of v1, /device:TPU:0, one launch (start us, length us, event | category | flops | bytes accessed | tf_op | source)
XLA Modules:
  0.0 122.8 jit_solution(13331875620122357936)
XLA Ops:
  0.6 3.5 %shard_map.84.h_ref = bf16[256,4096]{1,0:T(8,128)(2,1)} custom-call(bf16[256,4096]{1,0:T(8,128)(2,1)} %g_ref.5, bf16[256,4096]{1,0:T(8,128)(2,1)} %u_ref.5), custom_call_target="tpu_custom_call" | custom-call | flops 10485760 | bytes 6291456 | tf_op jit(solution)/shard_map/pallas_call | solution.py:61
  4.1 0.5 collective-permute-start.2
  4.7 2.6 %collective-permute-start.1 = (bf16[256,1024]{1,0:T(8,128)(2,1)}, bf16[256,1024]{1,0:T(8,128)(2,1)S(1)}, u32[]{:S(2)}, u32[]{:S(2)}) collective-permute-start(bf16[256,1024]{1,0:T(8,128)(2,1)} %refs_4_.3), channel_id=1, source_target_pairs={{4,0},{8,4},{12,8},{14,12},{10,14},{6,10},{2,6},{0,2},{5,1},{9,5},... | collective-permute-start | bytes 1572872 | tf_op jit(solution)/shard_map/ppermute | solution.py:565
  7.2 0.1 collective-permute-start
  7.4 0.1 pad_add_fusion.p_ref.refs_0_
  7.5 0.1 add_convert_fusion.7.f_ref.refs_1_
  7.6 1.2 collective-permute-done.2.x_ref
  8.8 1.6 %copy-done.1 = bf16[256,4096]{1,0:T(8,128)(2,1)S(1)} copy-done((bf16[256,4096]{1,0:T(8,128)(2,1)S(1)}, bf16[256,4096]{1,0:T(8,128)(2,1)}, u32[]{:S(2)}) %copy-start.1) | copy-done | bytes 2097176
  10.4 7.4 %shard_map.85 = (bf16[256,1024]{1,0:T(8,128)(2,1)S(1)}, bf16[256,1024]{1,0:T(8,128)(2,1)S(1)}, bf16[4096,512]{1,0:T(8,128)(2,1)S(1)}) custom-call(s32[1]{0:T(128)} %bitcast.p_ref.refs_0_, bf16[256,4096]{1,0:T(8,128)(2,1)S(1)} %copy-done.1, bf16[256,4096]{1,0:T(8,128)(2,1)} %collective-permute-done.2.x_ref, bf16[4096,4096]{1,0:T(8,128)(2,1)} %refs_15_.1, ...), custom_call_target="tpu_custom_call" | custom-call | flops 4294967296 | bytes 8388608 | tf_op jit(solution)/shard_map/pallas_call | solution.py:200
  17.8 2.2 %collective-permute-done.1.refs_1_ = bf16[256,1024]{1,0:T(8,128)(2,1)S(1)} collective-permute-done((bf16[256,1024]{1,0:T(8,128)(2,1)}, bf16[256,1024]{1,0:T(8,128)(2,1)S(1)}, u32[]{:S(2)}, u32[]{:S(2)}) %collective-permute-start.1) | collective-permute-done | bytes 524320 | tf_op jit(solution)/shard_map/ppermute | solution.py:565
  20.0 1.4 %collective-permute-done.refs_0_ = bf16[256,1024]{1,0:T(8,128)(2,1)S(1)} collective-permute-done((bf16[256,1024]{1,0:T(8,128)(2,1)}, bf16[256,1024]{1,0:T(8,128)(2,1)S(1)}, u32[]{:S(2)}, u32[]{:S(2)}) %collective-permute-start) | collective-permute-done | bytes 524320 | tf_op jit(solution)/shard_map/ppermute | solution.py:562
  21.4 0.4 collective-permute-start.3
  21.8 1.7 %collective-permute-start.4 = (bf16[256,1024]{1,0:T(8,128)(2,1)S(1)}, bf16[256,1024]{1,0:T(8,128)(2,1)S(1)}, u32[]{:S(2)}, u32[]{:S(2)}) collective-permute-start(bf16[256,1024]{1,0:T(8,128)(2,1)S(1)} %get-tuple-element.36.refs_1_.refs_2_.refs_6_.refs_18_.refs_10_), channel_id=1, source_target_pairs={{4,0},{8,4},{12,8},{14,12},{10,14},{6,10},{2,6},{0,2},{5,1},{9,5},... | collective-permute-start | bytes 1572872 | tf_op jit(solution)/shard_map/ppermute | solution.py:565
  23.5 0.0 collective-permute-start.7
  23.5 12.6 %shard_map.87 = (bf16[512,1024]{1,0:T(8,128)(2,1)S(1)}, bf16[512,1024]{1,0:T(8,128)(2,1)S(1)}) custom-call(s32[2]{0:T(128)S(1)} %pad_add_fusion.p_ref.refs_0_, bf16[256,4096]{1,0:T(8,128)(2,1)S(1)} %copy-done.1, bf16[256,4096]{1,0:T(8,128)(2,1)} %collective-permute-done.2.x_ref, bf16[4096,4096]{1,0:T(8,128)(2,1)} %refs_15_.1, s32[128,4096]{1,0:T(8,128)S(1)} %copy-done, ...), custom_call_target="tpu_custom_call" | custom-call | flops 8589934592 | bytes 16777216 | tf_op jit(solution)/shard_map/pallas_call | solution.py:200
  36.1 0.6 collective-permute-start.13
  36.7 0.0 collective-permute-done.3.refs_0_
  36.7 0.0 collective-permute-done.4.refs_1_
  36.7 0.4 collective-permute-start.5
  37.0 1.7 %collective-permute-start.6 = (bf16[256,1024]{1,0:T(8,128)(2,1)S(1)}, bf16[256,1024]{1,0:T(8,128)(2,1)S(1)}, u32[]{:S(2)}, u32[]{:S(2)}) collective-permute-start(bf16[256,1024]{1,0:T(8,128)(2,1)S(1)} %get-tuple-element.39.refs_1_.refs_2_.refs_20_.refs_12_), channel_id=1, source_target_pairs={{4,0},{8,4},{12,8},{14,12},{10,14},{6,10},{2,6},{0,2},{5,1},{9,5},... | collective-permute-start | bytes 1572872 | tf_op jit(solution)/shard_map/ppermute | solution.py:565
  38.7 0.2 shard_map.91
  38.9 0.1 collective-permute-start.10
  39.0 7.1 %shard_map.89 = (bf16[256,1024]{1,0:T(8,128)(2,1)S(1)}, bf16[256,1024]{1,0:T(8,128)(2,1)S(1)}) custom-call(s32[1]{0:T(128)} %bitcast.3.p_ref.refs_0_, bf16[256,4096]{1,0:T(8,128)(2,1)S(1)} %copy-done.1, bf16[256,4096]{1,0:T(8,128)(2,1)} %collective-permute-done.2.x_ref, bf16[4096,4096]{1,0:T(8,128)(2,1)} %refs_15_.1, s32[128,4096]{1,0:T(8,128)S(1)} %copy-done, ...), custom_call_target="tpu_custom_call" | custom-call | flops 4294967296 | bytes 8388608 | tf_op jit(solution)/shard_map/pallas_call | solution.py:200
  46.1 0.1 broadcast_select_fusion.refs_7_
  46.2 1.6 %collective-permute-start.9 = (bf16[128,1024]{1,0:T(8,128)(2,1)S(1)}, bf16[128,1024]{1,0:T(8,128)(2,1)S(1)}, u32[]{:S(2)}, u32[]{:S(2)}) collective-permute-start(bf16[128,1024]{1,0:T(8,128)(2,1)S(1)} %get-tuple-element.70), channel_id=1, source_target_pairs={{4,0},{8,4},{12,8},{14,12},{10,14},{6,10},{2,6},{0,2},{5,1},{9,5},... | collective-permute-start | bytes 786440 | tf_op jit(solution)/shard_map/ppermute | solution.py:565
  47.9 0.4 collective-permute-start.8
  48.3 7.5 %shard_map.92.refs_4_.refs_9_ = bf16[4096,4096]{1,0:T(8,128)(2,1)} custom-call(s32[1]{0:T(128)} %bitcast.3.p_ref.refs_0_, s32[1]{0:T(128)S(6)} %convert_element_type.82.f_ref.refs_1_, bf16[256,1024]{1,0:T(8,128)(2,1)S(1)} %get-tuple-element.39.refs_1_.refs_2_.refs_20_.refs_12_, bf16[256,1024]{1,0:T(8,128)(2,1)S(1)} %get-tuple-element.38.refs_0_.refs_3_.refs_21_.refs_13_, ...), custom_call_target="tpu_custom_call" | custom-call | flops 4294967296 | bytes 8388608 | tf_op jit(solution)/shard_map/pallas_call | solution.py:284
  55.8 0.5 collective-permute-done.9.refs_3_
  56.3 0.0 collective-permute-done.8.refs_2_
  56.3 0.0 collective-permute-done.5.refs_0_
  56.3 0.0 collective-permute-done.6.refs_1_
  56.3 0.7 shard_map.94
  57.0 0.1 collective-permute-start.16
  57.1 0.5 collective-permute-start.17
  57.6 1.7 %collective-permute-start.12 = (bf16[128,1024]{1,0:T(8,128)(2,1)S(1)}, bf16[128,1024]{1,0:T(8,128)(2,1)S(1)}, u32[]{:S(2)}, u32[]{:S(2)}) collective-permute-start(bf16[128,1024]{1,0:T(8,128)(2,1)S(1)} %slice.27), channel_id=1, source_target_pairs={{4,0},{8,4},{12,8},{14,12},{10,14},{6,10},{2,6},{0,2},{5,1},{9,5},... | collective-permute-start | bytes 786440 | tf_op jit(solution)/shard_map/ppermute | solution.py:565
  59.3 0.4 collective-permute-start.11
  59.7 0.0 collective-permute-done.13
  59.7 0.5 add_convert_fusion.5
  60.2 1.7 %collective-permute-start.15 = (bf16[256,1024]{1,0:T(8,128)(2,1)S(1)}, bf16[256,1024]{1,0:T(8,128)(2,1)S(1)}, u32[]{:S(2)}, u32[]{:S(2)}) collective-permute-start(bf16[256,1024]{1,0:T(8,128)(2,1)S(1)} %get-tuple-element.66.refs_11_), channel_id=1, source_target_pairs={{4,0},{8,4},{12,8},{14,12},{10,14},{6,10},{2,6},{0,2},{5,1},{9,5},... | collective-permute-start | bytes 1572872 | tf_op jit(solution)/shard_map/ppermute | solution.py:565
  61.9 0.4 collective-permute-start.14
  62.3 13.9 %shard_map.95.refs_4_.refs_7_ = bf16[4096,4096]{1,0:T(8,128)(2,1)} custom-call(s32[2]{0:T(128)S(1)} %pad_add_fusion.p_ref.refs_0_, s32[2]{0:T(128)S(1)} %add_convert_fusion.7.f_ref.refs_1_, bf16[256,1024]{1,0:T(8,128)(2,1)S(1)} %get-tuple-element.44.refs_1_.refs_2_.refs_14_.refs_6_, ...), custom_call_target="tpu_custom_call", output_to_operand_aliasing={{}: (9, {})} | custom-call | flops 8589934592 | bytes 16777216 | tf_op jit(solution)/shard_map/pallas_call | solution.py:284
  76.2 0.0 collective-permute-done.12.refs_1_
  76.2 1.0 collective-permute-done.15.refs_3_
  77.2 1.4 %collective-permute-done.14.refs_2_ = bf16[256,1024]{1,0:T(8,128)(2,1)S(1)} collective-permute-done((bf16[256,1024]{1,0:T(8,128)(2,1)S(1)}, bf16[256,1024]{1,0:T(8,128)(2,1)S(1)}, u32[]{:S(2)}, u32[]{:S(2)}) %collective-permute-start.14) | collective-permute-done | bytes 524320 | tf_op jit(solution)/shard_map/ppermute | solution.py:562
  78.6 0.1 collective-permute-start.20
  78.7 0.1 pad_add_fusion.1.refs_8_.refs_0_
  78.8 0.1 add_convert_fusion.8.refs_9_.refs_1_
  78.9 0.4 add_convert_fusion.3
  79.3 1.6 %collective-permute-start.19 = (bf16[256,1024]{1,0:T(8,128)(2,1)S(1)}, bf16[256,1024]{1,0:T(8,128)(2,1)S(1)}, u32[]{:S(2)}, u32[]{:S(2)}) collective-permute-start(bf16[256,1024]{1,0:T(8,128)(2,1)S(1)} %get-tuple-element.68.refs_26_), channel_id=1, source_target_pairs={{4,0},{8,4},{12,8},{14,12},{10,14},{6,10},{2,6},{0,2},{5,1},{9,5},... | collective-permute-start | bytes 1572872 | tf_op jit(solution)/shard_map/ppermute | solution.py:565
  81.0 0.4 collective-permute-start.18
  81.4 19.2 %shard_map.98 = (bf16[4096,4096]{1,0:T(8,128)(2,1)}, f32[256,2048]{1,0:T(8,128)S(1)}, bf16[256,2048]{1,0:T(8,128)(2,1)S(1)}) custom-call(s32[1]{0:T(128)} %bitcast.p_ref.refs_0_, s32[1]{0:T(128)S(6)} %convert_element_type.96.f_ref.refs_1_, bf16[128,1024]{1,0:T(8,128)(2,1)S(1)} %get-tuple-element.51.refs_1_.refs_2_.refs_10_, ...), custom_call_target="tpu_custom_call", output_to_operand_aliasing={{0}: (7, {})} | custom-call | flops 12884901888 | bytes 25165824 | tf_op jit(solution)/shard_map/pallas_call | solution.py:284
  100.6 0.1 collective-permute-start.24
  100.7 0.6 add_convert_fusion.2
  101.3 1.2 collective-permute-start.21
  102.5 0.9 collective-permute-start.22
  103.4 12.8 %shard_map.100 = (f32[256,2048]{1,0:T(8,128)S(1)}, bf16[256,2048]{1,0:T(8,128)(2,1)S(1)}) custom-call(s32[4]{0:T(128)S(1)} %pad_add_fusion.1.refs_8_.refs_0_, s32[4]{0:T(128)S(1)} %add_convert_fusion.8.refs_9_.refs_1_, bf16[128,1024]{1,0:T(8,128)(2,1)S(1)} %get-tuple-element.51.refs_1_.refs_2_.refs_10_, ...), custom_call_target="tpu_custom_call" | custom-call | flops 8589934592 | bytes 16777216 | tf_op jit(solution)/shard_map/pallas_call | solution.py:284
  116.3 0.0 copy-start.2
  116.3 0.1 collective-permute-start.23
  116.4 0.2 collective-permute-done.22
  116.6 0.4 add_convert_fusion.refs_2_
  117.0 0.0 copy-start.4
  117.0 0.9 copy-done.2
  117.9 2.5 %shard_map.101 = (bf16[256,4096]{1,0:T(8,128)(2,1)}, bf16[256,4096]{1,0:T(8,128)(2,1)}) custom-call(bf16[256,4096]{1,0:T(8,128)(2,1)S(1)} %copy-done.2, bf16[256,4096]{1,0:T(8,128)(2,1)S(1)} %copy-done.3, f32[256,2048]{1,0:T(8,128)S(1)} %get-tuple-element.58.m_ref, bf16[256,2048]{1,0:T(8,128)(2,1)S(1)} %collective-permute-done.24.o_ref, ...), custom_call_target="tpu_custom_call" | custom-call | flops 10485760000 | bytes 524288000 | tf_op jit(solution)/shard_map/pallas_call | solution.py:90
  120.3 2.5 %shard_map.102 = (bf16[256,4096]{1,0:T(8,128)(2,1)}, bf16[256,4096]{1,0:T(8,128)(2,1)}) custom-call(bf16[256,4096]{1,0:T(8,128)(2,1)S(1)} %copy-done.2, bf16[256,4096]{1,0:T(8,128)(2,1)S(1)} %copy-done.3, f32[256,2048]{1,0:T(8,128)S(1)} %get-tuple-element.56.m_ref, ...), custom_call_target="tpu_custom_call", output_to_operand_aliasing={{0}: (4, {}), {1}: (5, {})} | custom-call | flops 10485760000 | bytes 524288000 | tf_op jit(solution)/shard_map/pallas_call | solution.py:90
  (27 shorter events, 0.2 us)
Async XLA Ops:
  0.6 8.2 %copy-start = (s32[128,4096]{1,0:T(8,128)S(1)}, s32[128,4096]{1,0:T(8,128)}, u32[]{:S(2)}) copy-start(s32[128,4096]{1,0:T(8,128)} %refs_16_.1) | copy-start | bytes 6291460
  4.1 4.6 %collective-permute-start.2 = (bf16[256,4096]{1,0:T(8,128)(2,1)}, bf16[256,4096]{1,0:T(8,128)(2,1)}, u32[]{:S(2)}, u32[]{:S(2)}) collective-permute-start(bf16[256,4096]{1,0:T(8,128)(2,1)} %shard_map.84.h_ref), channel_id=1, source_target_pairs={{0,1},{1,0},{2,3},{3,2},{4,5},{5,4},{6,7},{7,6},{8,9},{9,8},{10,11... | collective-permute-start | bytes 6291464 | tf_op jit(solution)/shard_map/ppermute | solution.py:559
  4.7 15.4 %collective-permute-start.1 = (bf16[256,1024]{1,0:T(8,128)(2,1)}, bf16[256,1024]{1,0:T(8,128)(2,1)S(1)}, u32[]{:S(2)}, u32[]{:S(2)}) collective-permute-start(bf16[256,1024]{1,0:T(8,128)(2,1)} %refs_4_.3), channel_id=1, source_target_pairs={{4,0},{8,4},{12,8},{14,12},{10,14},{6,10},{2,6},{0,2},{5,1},{9,5},... | collective-permute-start | bytes 1572872 | tf_op jit(solution)/shard_map/ppermute | solution.py:565
  7.2 14.2 %collective-permute-start = (bf16[256,1024]{1,0:T(8,128)(2,1)}, bf16[256,1024]{1,0:T(8,128)(2,1)S(1)}, u32[]{:S(2)}, u32[]{:S(2)}) collective-permute-start(bf16[256,1024]{1,0:T(8,128)(2,1)} %refs_4_.3), channel_id=1, source_target_pairs={{0,4},{4,8},{8,12},{12,14},{14,10},{10,6},{6,2},{2,0},{1,5},{5,9},... | collective-permute-start | bytes 1572872 | tf_op jit(solution)/shard_map/ppermute | solution.py:562
  8.8 1.6 %copy-start.1 = (bf16[256,4096]{1,0:T(8,128)(2,1)S(1)}, bf16[256,4096]{1,0:T(8,128)(2,1)}, u32[]{:S(2)}) copy-start(bf16[256,4096]{1,0:T(8,128)(2,1)} %shard_map.84.h_ref) | copy-start | bytes 6291460
  21.4 15.2 %collective-permute-start.3 = (bf16[256,1024]{1,0:T(8,128)(2,1)S(1)}, bf16[256,1024]{1,0:T(8,128)(2,1)S(1)}, u32[]{:S(2)}, u32[]{:S(2)}) collective-permute-start(bf16[256,1024]{1,0:T(8,128)(2,1)S(1)} %get-tuple-element.35.refs_0_.refs_3_.refs_15_.refs_7_), channel_id=1, source_target_pairs={{0,4},{4,8},{8,12},{12,14},{14,10},{10,6},{6,2},{2,0},{1,5},{5,9},... | collective-permute-start | bytes 1572872 | tf_op jit(solution)/shard_map/ppermute | solution.py:562
  21.8 14.9 %collective-permute-start.4 = (bf16[256,1024]{1,0:T(8,128)(2,1)S(1)}, bf16[256,1024]{1,0:T(8,128)(2,1)S(1)}, u32[]{:S(2)}, u32[]{:S(2)}) collective-permute-start(bf16[256,1024]{1,0:T(8,128)(2,1)S(1)} %get-tuple-element.36.refs_1_.refs_2_.refs_6_.refs_18_.refs_10_), channel_id=1, source_target_pairs={{4,0},{8,4},{12,8},{14,12},{10,14},{6,10},{2,6},{0,2},{5,1},{9,5},... | collective-permute-start | bytes 1572872 | tf_op jit(solution)/shard_map/ppermute | solution.py:565
  23.5 22.6 %collective-permute-start.7 = (bf16[256,1024]{1,0:T(8,128)(2,1)S(1)}, bf16[256,1024]{1,0:T(8,128)(2,1)S(1)}, u32[]{:S(2)}, u32[]{:S(2)}) collective-permute-start(bf16[256,1024]{1,0:T(8,128)(2,1)S(1)} %get-tuple-element.40), channel_id=1, source_target_pairs={{0,1},{1,0},{2,3},{3,2},{4,5},{5,4},{6,7},{7,6},{8,9},{9,8},{10,11... | collective-permute-start | bytes 1572872 | tf_op jit(solution)/shard_map/ppermute | solution.py:559
  36.1 23.6 %collective-permute-start.13 = (bf16[512,1024]{1,0:T(8,128)(2,1)S(1)}, bf16[512,1024]{1,0:T(8,128)(2,1)S(1)}, u32[]{:S(2)}, u32[]{:S(2)}) collective-permute-start(bf16[512,1024]{1,0:T(8,128)(2,1)S(1)} %get-tuple-element.46), channel_id=1, source_target_pairs={{0,1},{1,0},{2,3},{3,2},{4,5},{5,4},{6,7},{7,6},{8,9},{9,8},{10,11... | collective-permute-start | bytes 3145736 | tf_op jit(solution)/shard_map/ppermute | solution.py:559
  36.7 19.6 %collective-permute-start.5 = (bf16[256,1024]{1,0:T(8,128)(2,1)S(1)}, bf16[256,1024]{1,0:T(8,128)(2,1)S(1)}, u32[]{:S(2)}, u32[]{:S(2)}) collective-permute-start(bf16[256,1024]{1,0:T(8,128)(2,1)S(1)} %get-tuple-element.38.refs_0_.refs_3_.refs_21_.refs_13_), channel_id=1, source_target_pairs={{0,4},{4,8},{8,12},{12,14},{14,10},{10,6},{6,2},{2,0},{1,5},{5,9},... | collective-permute-start | bytes 1572872 | tf_op jit(solution)/shard_map/ppermute | solution.py:562
  37.0 19.3 %collective-permute-start.6 = (bf16[256,1024]{1,0:T(8,128)(2,1)S(1)}, bf16[256,1024]{1,0:T(8,128)(2,1)S(1)}, u32[]{:S(2)}, u32[]{:S(2)}) collective-permute-start(bf16[256,1024]{1,0:T(8,128)(2,1)S(1)} %get-tuple-element.39.refs_1_.refs_2_.refs_20_.refs_12_), channel_id=1, source_target_pairs={{4,0},{8,4},{12,8},{14,12},{10,14},{6,10},{2,6},{0,2},{5,1},{9,5},... | collective-permute-start | bytes 1572872 | tf_op jit(solution)/shard_map/ppermute | solution.py:565
  38.9 8.9 %collective-permute-start.10 = (bf16[256,1024]{1,0:T(8,128)(2,1)S(1)}, bf16[256,1024]{1,0:T(8,128)(2,1)S(1)}, u32[]{:S(2)}, u32[]{:S(2)}) collective-permute-start(bf16[256,1024]{1,0:T(8,128)(2,1)S(1)} %shard_map.91), channel_id=1, source_target_pairs={{0,1},{1,0},{2,3},{3,2},{4,5},{5,4},{6,7},{7,6},{8,9},{9,8},{10,11... | collective-permute-start | bytes 1572872 | tf_op jit(solution)/shard_map/ppermute | solution.py:559
  46.2 10.1 %collective-permute-start.9 = (bf16[128,1024]{1,0:T(8,128)(2,1)S(1)}, bf16[128,1024]{1,0:T(8,128)(2,1)S(1)}, u32[]{:S(2)}, u32[]{:S(2)}) collective-permute-start(bf16[128,1024]{1,0:T(8,128)(2,1)S(1)} %get-tuple-element.70), channel_id=1, source_target_pairs={{4,0},{8,4},{12,8},{14,12},{10,14},{6,10},{2,6},{0,2},{5,1},{9,5},... | collective-permute-start | bytes 786440 | tf_op jit(solution)/shard_map/ppermute | solution.py:565
  47.9 8.4 %collective-permute-start.8 = (bf16[128,1024]{1,0:T(8,128)(2,1)S(1)}, bf16[128,1024]{1,0:T(8,128)(2,1)S(1)}, u32[]{:S(2)}, u32[]{:S(2)}) collective-permute-start(bf16[128,1024]{1,0:T(8,128)(2,1)S(1)} %get-tuple-element.71), channel_id=1, source_target_pairs={{0,4},{4,8},{8,12},{12,14},{14,10},{10,6},{6,2},{2,0},{1,5},{5,9},... | collective-permute-start | bytes 786440 | tf_op jit(solution)/shard_map/ppermute | solution.py:562
  57.0 4.9 %collective-permute-start.16 = (bf16[512,1024]{1,0:T(8,128)(2,1)S(1)}, bf16[512,1024]{1,0:T(8,128)(2,1)S(1)}, u32[]{:S(2)}, u32[]{:S(2)}) collective-permute-start(bf16[512,1024]{1,0:T(8,128)(2,1)S(1)} %shard_map.94), channel_id=1, source_target_pairs={{0,1},{1,0},{2,3},{3,2},{4,5},{5,4},{6,7},{7,6},{8,9},{9,8},{10,11... | collective-permute-start | bytes 3145736 | tf_op jit(solution)/shard_map/ppermute | solution.py:559
  57.1 21.8 %collective-permute-start.17 = (bf16[256,1024]{1,0:T(8,128)(2,1)S(1)}, bf16[256,1024]{1,0:T(8,128)(2,1)S(1)}, u32[]{:S(2)}, u32[]{:S(2)}) collective-permute-start(bf16[256,1024]{1,0:T(8,128)(2,1)S(1)} %get-tuple-element.49), channel_id=1, source_target_pairs={{0,1},{1,0},{2,3},{3,2},{4,5},{5,4},{6,7},{7,6},{8,9},{9,8},{10,11... | collective-permute-start | bytes 1572872 | tf_op jit(solution)/shard_map/ppermute | solution.py:559
  57.6 18.5 %collective-permute-start.12 = (bf16[128,1024]{1,0:T(8,128)(2,1)S(1)}, bf16[128,1024]{1,0:T(8,128)(2,1)S(1)}, u32[]{:S(2)}, u32[]{:S(2)}) collective-permute-start(bf16[128,1024]{1,0:T(8,128)(2,1)S(1)} %slice.27), channel_id=1, source_target_pairs={{4,0},{8,4},{12,8},{14,12},{10,14},{6,10},{2,6},{0,2},{5,1},{9,5},... | collective-permute-start | bytes 786440 | tf_op jit(solution)/shard_map/ppermute | solution.py:565
  59.3 16.8 %collective-permute-start.11 = (bf16[128,1024]{1,0:T(8,128)(2,1)S(1)}, bf16[128,1024]{1,0:T(8,128)(2,1)S(1)}, u32[]{:S(2)}, u32[]{:S(2)}) collective-permute-start(bf16[128,1024]{1,0:T(8,128)(2,1)S(1)} %slice.26), channel_id=1, source_target_pairs={{0,4},{4,8},{8,12},{12,14},{14,10},{10,6},{6,2},{2,0},{1,5},{5,9},... | collective-permute-start | bytes 786440 | tf_op jit(solution)/shard_map/ppermute | solution.py:562
  60.2 17.0 %collective-permute-start.15 = (bf16[256,1024]{1,0:T(8,128)(2,1)S(1)}, bf16[256,1024]{1,0:T(8,128)(2,1)S(1)}, u32[]{:S(2)}, u32[]{:S(2)}) collective-permute-start(bf16[256,1024]{1,0:T(8,128)(2,1)S(1)} %get-tuple-element.66.refs_11_), channel_id=1, source_target_pairs={{4,0},{8,4},{12,8},{14,12},{10,14},{6,10},{2,6},{0,2},{5,1},{9,5},... | collective-permute-start | bytes 1572872 | tf_op jit(solution)/shard_map/ppermute | solution.py:565
  61.9 16.6 %collective-permute-start.14 = (bf16[256,1024]{1,0:T(8,128)(2,1)S(1)}, bf16[256,1024]{1,0:T(8,128)(2,1)S(1)}, u32[]{:S(2)}, u32[]{:S(2)}) collective-permute-start(bf16[256,1024]{1,0:T(8,128)(2,1)S(1)} %get-tuple-element.67.refs_10_), channel_id=1, source_target_pairs={{0,4},{4,8},{8,12},{12,14},{14,10},{10,6},{6,2},{2,0},{1,5},{5,9},... | collective-permute-start | bytes 1572872 | tf_op jit(solution)/shard_map/ppermute | solution.py:562
  78.6 2.8 %collective-permute-start.20 = (bf16[256,1024]{1,0:T(8,128)(2,1)S(1)}, bf16[256,1024]{1,0:T(8,128)(2,1)S(1)}, u32[]{:S(2)}, u32[]{:S(2)}) collective-permute-start(bf16[256,1024]{1,0:T(8,128)(2,1)S(1)} %shard_map.97), channel_id=1, source_target_pairs={{0,1},{1,0},{2,3},{3,2},{4,5},{5,4},{6,7},{7,6},{8,9},{9,8},{10,11... | collective-permute-start | bytes 1572872 | tf_op jit(solution)/shard_map/ppermute | solution.py:559
  79.3 21.3 %collective-permute-start.19 = (bf16[256,1024]{1,0:T(8,128)(2,1)S(1)}, bf16[256,1024]{1,0:T(8,128)(2,1)S(1)}, u32[]{:S(2)}, u32[]{:S(2)}) collective-permute-start(bf16[256,1024]{1,0:T(8,128)(2,1)S(1)} %get-tuple-element.68.refs_26_), channel_id=1, source_target_pairs={{4,0},{8,4},{12,8},{14,12},{10,14},{6,10},{2,6},{0,2},{5,1},{9,5},... | collective-permute-start | bytes 1572872 | tf_op jit(solution)/shard_map/ppermute | solution.py:565
  81.0 19.7 %collective-permute-start.18 = (bf16[256,1024]{1,0:T(8,128)(2,1)S(1)}, bf16[256,1024]{1,0:T(8,128)(2,1)S(1)}, u32[]{:S(2)}, u32[]{:S(2)}) collective-permute-start(bf16[256,1024]{1,0:T(8,128)(2,1)S(1)} %get-tuple-element.69.refs_25_), channel_id=1, source_target_pairs={{0,4},{4,8},{8,12},{12,14},{14,10},{10,6},{6,2},{2,0},{1,5},{5,9},... | collective-permute-start | bytes 1572872 | tf_op jit(solution)/shard_map/ppermute | solution.py:562
  100.6 16.4 %collective-permute-start.24 = (bf16[256,2048]{1,0:T(8,128)(2,1)S(1)}, bf16[256,2048]{1,0:T(8,128)(2,1)S(1)}, u32[]{:S(2)}, u32[]{:S(2)}) collective-permute-start(bf16[256,2048]{1,0:T(8,128)(2,1)S(1)} %get-tuple-element.53.refs_2_), channel_id=1, source_target_pairs={{0,1},{1,0},{2,3},{3,2},{4,5},{5,4},{6,7},{7,6},{8,9},{9,8},{10,11... | collective-permute-start | bytes 3145736 | tf_op jit(solution)/shard_map/ppermute | solution.py:559
  101.3 15.0 %collective-permute-start.21 = (bf16[256,1024]{1,0:T(8,128)(2,1)S(1)}, bf16[256,1024]{1,0:T(8,128)(2,1)S(1)}, u32[]{:S(2)}, u32[]{:S(2)}) collective-permute-start(bf16[256,1024]{1,0:T(8,128)(2,1)S(1)} %get-tuple-element.64.refs_17_), channel_id=1, source_target_pairs={{0,4},{4,8},{8,12},{12,14},{14,10},{10,6},{6,2},{2,0},{1,5},{5,9},... | collective-permute-start | bytes 1572872 | tf_op jit(solution)/shard_map/ppermute | solution.py:562
  102.5 14.1 %collective-permute-start.22 = (bf16[256,1024]{1,0:T(8,128)(2,1)S(1)}, bf16[256,1024]{1,0:T(8,128)(2,1)S(1)}, u32[]{:S(2)}, u32[]{:S(2)}) collective-permute-start(bf16[256,1024]{1,0:T(8,128)(2,1)S(1)} %get-tuple-element.65.refs_18_), channel_id=1, source_target_pairs={{4,0},{8,4},{12,8},{14,12},{10,14},{6,10},{2,6},{0,2},{5,1},{9,5},... | collective-permute-start | bytes 1572872 | tf_op jit(solution)/shard_map/ppermute | solution.py:565
  103.4 13.6 %copy-start.3 = (bf16[256,4096]{1,0:T(8,128)(2,1)S(1)}, bf16[256,4096]{1,0:T(8,128)(2,1)}, u32[]{:S(2)}) copy-start(bf16[256,4096]{1,0:T(8,128)(2,1)} %u_ref.5) | copy-start | bytes 6291460
  116.3 1.6 %copy-start.2 = (bf16[256,4096]{1,0:T(8,128)(2,1)S(1)}, bf16[256,4096]{1,0:T(8,128)(2,1)}, u32[]{:S(2)}) copy-start(bf16[256,4096]{1,0:T(8,128)(2,1)} %g_ref.5) | copy-start | bytes 6291460
  116.3 4.1 %collective-permute-start.23 = (bf16[256,2048]{1,0:T(8,128)(2,1)S(1)}, bf16[256,2048]{1,0:T(8,128)(2,1)S(1)}, u32[]{:S(2)}, u32[]{:S(2)}) collective-permute-start(bf16[256,2048]{1,0:T(8,128)(2,1)S(1)} %get-tuple-element.57.refs_0_), channel_id=1, source_target_pairs={{0,1},{1,0},{2,3},{3,2},{4,5},{5,4},{6,7},{7,6},{8,9},{9,8},{10,11... | collective-permute-start | bytes 3145736 | tf_op jit(solution)/shard_map/ppermute | solution.py:559
  117.0 3.4 %copy-start.4 = (bf16[256,1024]{1,0:T(8,128)(2,1)}, bf16[256,1024]{1,0:T(8,128)(2,1)S(1)}, u32[]{:S(2)}) copy-start(bf16[256,1024]{1,0:T(8,128)(2,1)S(1)} %add_convert_fusion.refs_2_) | copy-start | bytes 1572868

commit v2 on v1

--- a/solution.py
+++ b/solution.py
@@ -79,7 +79,7 @@
         dg_ref, du_ref = refs[-2:]
         value = g_ref[...].astype(F32)
         s = sigmoid(value)
-        grad = m_ref[...] + o_ref[...].astype(F32)
+        grad = m_ref[...].astype(F32) + o_ref[...].astype(F32)
         slope = s * (1.0 + value * (1.0 - s))
         dg_ref[...] = (grad * u_ref[...].astype(F32) * slope).astype(BF16)
         du_ref[...] = (grad * (value * s)).astype(BF16)
@@ -360,7 +360,7 @@
                 for copy in stores(i - 2):
                     copy.wait()
 
-            m_held[i % 2] = total[:tokens]
+            m_held[i % 2] = total[:tokens].astype(BF16)
             o_held[i % 2] = total[tokens:].astype(BF16)
             for copy in stores(i):
                 copy.start()
@@ -389,13 +389,13 @@
         scalars=2,
         numbers=[places, flags],
         inputs=[*slots.arrays, codes, exponents],
-        shapes=[jax.ShapeDtypeStruct((tokens, width), F32), jax.ShapeDtypeStruct((tokens, width), BF16)],
+        shapes=[jax.ShapeDtypeStruct((tokens, width), BF16)] * 2,
         aliases={},
         scratch=slots.scratch()
         + [
             pltpu.VMEM((2, count, tile, part), BF16),
             pltpu.VMEM((count, width // 32, part), jnp.int32),
-            pltpu.VMEM((2, tokens, tile), F32),
+            pltpu.VMEM((2, tokens, tile), BF16),
             pltpu.VMEM((2, tokens, tile), BF16),
             pltpu.SemaphoreType.DMA((2, count)),
             pltpu.SemaphoreType.DMA((count,)),

time: 123 us -> 123 us (level)
  no operation moved by 1% of the time
where the time goes in v2:
time: 123 us
  Pallas kernels  89.6 us (73%)
  starting transfers between devices  19.1 us (16%)
  waiting for transfers between devices  8.18 us (7%)
  local copies, waits for them, and re-layouts  2.42 us (2%)
  other arithmetic  2.32 us (2%)
    pallas_call x4, Pallas kernels, run(): pl.pallas_call(body, in_specs=[spec for p in phases for spec in [smem] *...  53.1 us
    pallas_call x3, Pallas kernels, output_terms(): pl.pallas_call(body, in_specs=[pl.BlockSpec(memory_space=pltpu.SMEM)] + [...  27.1 us
    ppermute x8, starting transfers between devices, back(): return lax.ppermute(value, 'grid', backward)  13.5 us
    pallas_call x2, Pallas kernels, finish(): pl.pallas_call(body, grid=(width // tile,), in_specs=[there, there, here,...  4.97 us
    ppermute x8, waiting for transfers between devices, back(): return lax.ppermute(value, 'grid', backward)  4.15 us
    ppermute x8, starting transfers between devices, on(): return lax.ppermute(value, 'grid', forward)  3.64 us
    pallas_call x1, Pallas kernels, make_hidden(): pl.pallas_call(body, in_specs=[ANY] * 2, out_specs=ANY, out_shape=jax.Sha...  3.5 us
    ppermute x8, waiting for transfers between devices, on(): return lax.ppermute(value, 'grid', forward)  2.81 us
  transfers between devices with their start and end apart: 25, of which 7 were waited for; matrix products, arithmetic and copies ran while one was open for 2% of the time, Pallas kernels for 68%

profile of v2, /device:TPU:0, one launch (start us, length us, event | category | flops | bytes accessed | tf_op | source)
XLA Modules:
  0.0 122.6 jit_solution(16508848546415320828)
XLA Ops:
  0.6 3.5 %shard_map.84.h_ref = bf16[256,4096]{1,0:T(8,128)(2,1)} custom-call(bf16[256,4096]{1,0:T(8,128)(2,1)} %g_ref.5, bf16[256,4096]{1,0:T(8,128)(2,1)} %u_ref.5), custom_call_target="tpu_custom_call" | custom-call | flops 10485760 | bytes 6291456 | tf_op jit(solution)/shard_map/pallas_call | solution.py:61
  4.1 0.5 collective-permute-start.2
  4.7 2.6 %collective-permute-start.1 = (bf16[256,1024]{1,0:T(8,128)(2,1)}, bf16[256,1024]{1,0:T(8,128)(2,1)S(1)}, u32[]{:S(2)}, u32[]{:S(2)}) collective-permute-start(bf16[256,1024]{1,0:T(8,128)(2,1)} %refs_4_.3), channel_id=1, source_target_pairs={{4,0},{8,4},{12,8},{14,12},{10,14},{6,10},{2,6},{0,2},{5,1},{9,5},... | collective-permute-start | bytes 1572872 | tf_op jit(solution)/shard_map/ppermute | solution.py:565
  7.2 0.1 collective-permute-start
  7.4 0.1 pad_add_fusion.p_ref.refs_0_
  7.5 0.1 add_convert_fusion.7.f_ref.refs_1_
  7.6 1.2 collective-permute-done.2.x_ref
  8.8 1.6 %copy-done.1 = bf16[256,4096]{1,0:T(8,128)(2,1)S(1)} copy-done((bf16[256,4096]{1,0:T(8,128)(2,1)S(1)}, bf16[256,4096]{1,0:T(8,128)(2,1)}, u32[]{:S(2)}) %copy-start.1) | copy-done | bytes 2097176
  10.4 7.4 %shard_map.85 = (bf16[256,1024]{1,0:T(8,128)(2,1)S(1)}, bf16[256,1024]{1,0:T(8,128)(2,1)S(1)}, bf16[4096,512]{1,0:T(8,128)(2,1)S(1)}) custom-call(s32[1]{0:T(128)} %bitcast.p_ref.refs_0_, bf16[256,4096]{1,0:T(8,128)(2,1)S(1)} %copy-done.1, bf16[256,4096]{1,0:T(8,128)(2,1)} %collective-permute-done.2.x_ref, bf16[4096,4096]{1,0:T(8,128)(2,1)} %refs_15_.1, ...), custom_call_target="tpu_custom_call" | custom-call | flops 4294967296 | bytes 8388608 | tf_op jit(solution)/shard_map/pallas_call | solution.py:200
  17.8 2.2 %collective-permute-done.1.refs_1_ = bf16[256,1024]{1,0:T(8,128)(2,1)S(1)} collective-permute-done((bf16[256,1024]{1,0:T(8,128)(2,1)}, bf16[256,1024]{1,0:T(8,128)(2,1)S(1)}, u32[]{:S(2)}, u32[]{:S(2)}) %collective-permute-start.1) | collective-permute-done | bytes 524320 | tf_op jit(solution)/shard_map/ppermute | solution.py:565
  20.0 1.4 %collective-permute-done.refs_0_ = bf16[256,1024]{1,0:T(8,128)(2,1)S(1)} collective-permute-done((bf16[256,1024]{1,0:T(8,128)(2,1)}, bf16[256,1024]{1,0:T(8,128)(2,1)S(1)}, u32[]{:S(2)}, u32[]{:S(2)}) %collective-permute-start) | collective-permute-done | bytes 524320 | tf_op jit(solution)/shard_map/ppermute | solution.py:562
  21.4 0.4 collective-permute-start.3
  21.8 1.7 %collective-permute-start.4 = (bf16[256,1024]{1,0:T(8,128)(2,1)S(1)}, bf16[256,1024]{1,0:T(8,128)(2,1)S(1)}, u32[]{:S(2)}, u32[]{:S(2)}) collective-permute-start(bf16[256,1024]{1,0:T(8,128)(2,1)S(1)} %get-tuple-element.36.refs_1_.refs_2_.refs_6_.refs_18_.refs_10_), channel_id=1, source_target_pairs={{4,0},{8,4},{12,8},{14,12},{10,14},{6,10},{2,6},{0,2},{5,1},{9,5},... | collective-permute-start | bytes 1572872 | tf_op jit(solution)/shard_map/ppermute | solution.py:565
  23.5 0.0 collective-permute-start.7
  23.5 12.6 %shard_map.87 = (bf16[512,1024]{1,0:T(8,128)(2,1)S(1)}, bf16[512,1024]{1,0:T(8,128)(2,1)S(1)}) custom-call(s32[2]{0:T(128)S(1)} %pad_add_fusion.p_ref.refs_0_, bf16[256,4096]{1,0:T(8,128)(2,1)S(1)} %copy-done.1, bf16[256,4096]{1,0:T(8,128)(2,1)} %collective-permute-done.2.x_ref, bf16[4096,4096]{1,0:T(8,128)(2,1)} %refs_15_.1, s32[128,4096]{1,0:T(8,128)S(1)} %copy-done, ...), custom_call_target="tpu_custom_call" | custom-call | flops 8589934592 | bytes 16777216 | tf_op jit(solution)/shard_map/pallas_call | solution.py:200
  36.1 0.6 collective-permute-start.13
  36.7 0.0 collective-permute-done.3.refs_0_
  36.7 0.0 collective-permute-done.4.refs_1_
  36.7 0.4 collective-permute-start.5
  37.0 1.7 %collective-permute-start.6 = (bf16[256,1024]{1,0:T(8,128)(2,1)S(1)}, bf16[256,1024]{1,0:T(8,128)(2,1)S(1)}, u32[]{:S(2)}, u32[]{:S(2)}) collective-permute-start(bf16[256,1024]{1,0:T(8,128)(2,1)S(1)} %get-tuple-element.39.refs_1_.refs_2_.refs_20_.refs_12_), channel_id=1, source_target_pairs={{4,0},{8,4},{12,8},{14,12},{10,14},{6,10},{2,6},{0,2},{5,1},{9,5},... | collective-permute-start | bytes 1572872 | tf_op jit(solution)/shard_map/ppermute | solution.py:565
  38.7 0.2 shard_map.91
  38.9 0.1 collective-permute-start.10
  39.0 7.1 %shard_map.89 = (bf16[256,1024]{1,0:T(8,128)(2,1)S(1)}, bf16[256,1024]{1,0:T(8,128)(2,1)S(1)}) custom-call(s32[1]{0:T(128)} %bitcast.3.p_ref.refs_0_, bf16[256,4096]{1,0:T(8,128)(2,1)S(1)} %copy-done.1, bf16[256,4096]{1,0:T(8,128)(2,1)} %collective-permute-done.2.x_ref, bf16[4096,4096]{1,0:T(8,128)(2,1)} %refs_15_.1, s32[128,4096]{1,0:T(8,128)S(1)} %copy-done, ...), custom_call_target="tpu_custom_call" | custom-call | flops 4294967296 | bytes 8388608 | tf_op jit(solution)/shard_map/pallas_call | solution.py:200
  46.1 0.1 broadcast_select_fusion.refs_7_
  46.2 1.6 %collective-permute-start.9 = (bf16[128,1024]{1,0:T(8,128)(2,1)S(1)}, bf16[128,1024]{1,0:T(8,128)(2,1)S(1)}, u32[]{:S(2)}, u32[]{:S(2)}) collective-permute-start(bf16[128,1024]{1,0:T(8,128)(2,1)S(1)} %get-tuple-element.70), channel_id=1, source_target_pairs={{4,0},{8,4},{12,8},{14,12},{10,14},{6,10},{2,6},{0,2},{5,1},{9,5},... | collective-permute-start | bytes 786440 | tf_op jit(solution)/shard_map/ppermute | solution.py:565
  47.9 0.4 collective-permute-start.8
  48.3 7.5 %shard_map.92.refs_4_.refs_9_ = bf16[4096,4096]{1,0:T(8,128)(2,1)} custom-call(s32[1]{0:T(128)} %bitcast.3.p_ref.refs_0_, s32[1]{0:T(128)S(6)} %convert_element_type.82.f_ref.refs_1_, bf16[256,1024]{1,0:T(8,128)(2,1)S(1)} %get-tuple-element.39.refs_1_.refs_2_.refs_20_.refs_12_, bf16[256,1024]{1,0:T(8,128)(2,1)S(1)} %get-tuple-element.38.refs_0_.refs_3_.refs_21_.refs_13_, ...), custom_call_target="tpu_custom_call" | custom-call | flops 4294967296 | bytes 8388608 | tf_op jit(solution)/shard_map/pallas_call | solution.py:284
  55.8 0.5 collective-permute-done.9.refs_3_
  56.3 0.0 collective-permute-done.8.refs_2_
  56.3 0.0 collective-permute-done.5.refs_0_
  56.3 0.0 collective-permute-done.6.refs_1_
  56.3 0.7 shard_map.94
  57.0 0.1 collective-permute-start.16
  57.1 0.5 collective-permute-start.17
  57.6 1.7 %collective-permute-start.12 = (bf16[128,1024]{1,0:T(8,128)(2,1)S(1)}, bf16[128,1024]{1,0:T(8,128)(2,1)S(1)}, u32[]{:S(2)}, u32[]{:S(2)}) collective-permute-start(bf16[128,1024]{1,0:T(8,128)(2,1)S(1)} %slice.27), channel_id=1, source_target_pairs={{4,0},{8,4},{12,8},{14,12},{10,14},{6,10},{2,6},{0,2},{5,1},{9,5},... | collective-permute-start | bytes 786440 | tf_op jit(solution)/shard_map/ppermute | solution.py:565
  59.3 0.4 collective-permute-start.11
  59.7 0.0 collective-permute-done.13
  59.7 0.5 add_convert_fusion.5
  60.2 1.7 %collective-permute-start.15 = (bf16[256,1024]{1,0:T(8,128)(2,1)S(1)}, bf16[256,1024]{1,0:T(8,128)(2,1)S(1)}, u32[]{:S(2)}, u32[]{:S(2)}) collective-permute-start(bf16[256,1024]{1,0:T(8,128)(2,1)S(1)} %get-tuple-element.66.refs_11_), channel_id=1, source_target_pairs={{4,0},{8,4},{12,8},{14,12},{10,14},{6,10},{2,6},{0,2},{5,1},{9,5},... | collective-permute-start | bytes 1572872 | tf_op jit(solution)/shard_map/ppermute | solution.py:565
  61.9 0.4 collective-permute-start.14
  62.3 13.9 %shard_map.95.refs_4_.refs_7_ = bf16[4096,4096]{1,0:T(8,128)(2,1)} custom-call(s32[2]{0:T(128)S(1)} %pad_add_fusion.p_ref.refs_0_, s32[2]{0:T(128)S(1)} %add_convert_fusion.7.f_ref.refs_1_, bf16[256,1024]{1,0:T(8,128)(2,1)S(1)} %get-tuple-element.44.refs_1_.refs_2_.refs_14_.refs_6_, ...), custom_call_target="tpu_custom_call", output_to_operand_aliasing={{}: (9, {})} | custom-call | flops 8589934592 | bytes 16777216 | tf_op jit(solution)/shard_map/pallas_call | solution.py:284
  76.2 0.0 collective-permute-done.12.refs_1_
  76.2 1.0 collective-permute-done.15.refs_3_
  77.2 1.4 %collective-permute-done.14.refs_2_ = bf16[256,1024]{1,0:T(8,128)(2,1)S(1)} collective-permute-done((bf16[256,1024]{1,0:T(8,128)(2,1)S(1)}, bf16[256,1024]{1,0:T(8,128)(2,1)S(1)}, u32[]{:S(2)}, u32[]{:S(2)}) %collective-permute-start.14) | collective-permute-done | bytes 524320 | tf_op jit(solution)/shard_map/ppermute | solution.py:562
  78.6 0.1 collective-permute-start.20
  78.7 0.1 pad_add_fusion.1.refs_8_.refs_0_
  78.8 0.1 add_convert_fusion.8.refs_9_.refs_1_
  78.9 0.4 add_convert_fusion.3
  79.3 1.6 %collective-permute-start.19 = (bf16[256,1024]{1,0:T(8,128)(2,1)S(1)}, bf16[256,1024]{1,0:T(8,128)(2,1)S(1)}, u32[]{:S(2)}, u32[]{:S(2)}) collective-permute-start(bf16[256,1024]{1,0:T(8,128)(2,1)S(1)} %get-tuple-element.68.refs_26_), channel_id=1, source_target_pairs={{4,0},{8,4},{12,8},{14,12},{10,14},{6,10},{2,6},{0,2},{5,1},{9,5},... | collective-permute-start | bytes 1572872 | tf_op jit(solution)/shard_map/ppermute | solution.py:565
  81.0 0.4 collective-permute-start.18
  81.4 19.0 %shard_map.98 = (bf16[4096,4096]{1,0:T(8,128)(2,1)}, bf16[256,2048]{1,0:T(8,128)(2,1)S(1)}, bf16[256,2048]{1,0:T(8,128)(2,1)S(1)}) custom-call(s32[1]{0:T(128)} %bitcast.p_ref.refs_0_, s32[1]{0:T(128)S(6)} %convert_element_type.96.f_ref.refs_1_, bf16[128,1024]{1,0:T(8,128)(2,1)S(1)} %get-tuple-element.51.refs_1_.refs_2_.refs_10_, ...), custom_call_target="tpu_custom_call", output_to_operand_aliasing={{0}: (7, {})} | custom-call | flops 12884901888 | bytes 25165824 | tf_op jit(solution)/shard_map/pallas_call | solution.py:284
  100.4 0.1 collective-permute-start.24
  100.6 0.6 add_convert_fusion.2
  101.2 1.2 collective-permute-start.21
  102.4 0.9 collective-permute-start.22
  103.3 12.7 %shard_map.100 = (bf16[256,2048]{1,0:T(8,128)(2,1)S(1)}, bf16[256,2048]{1,0:T(8,128)(2,1)S(1)}) custom-call(s32[4]{0:T(128)S(1)} %pad_add_fusion.1.refs_8_.refs_0_, s32[4]{0:T(128)S(1)} %add_convert_fusion.8.refs_9_.refs_1_, bf16[128,1024]{1,0:T(8,128)(2,1)S(1)} %get-tuple-element.51.refs_1_.refs_2_.refs_10_, ...), custom_call_target="tpu_custom_call" | custom-call | flops 8589934592 | bytes 16777216 | tf_op jit(solution)/shard_map/pallas_call | solution.py:284
  116.0 0.0 copy-start.2
  116.0 0.1 collective-permute-start.23
  116.1 0.4 collective-permute-done.22
  116.5 0.4 add_convert_fusion.refs_2_
  116.8 0.0 copy-start.4
  116.9 0.7 copy-done.2
  117.6 2.5 %shard_map.101 = (bf16[256,4096]{1,0:T(8,128)(2,1)}, bf16[256,4096]{1,0:T(8,128)(2,1)}) custom-call(bf16[256,4096]{1,0:T(8,128)(2,1)S(1)} %copy-done.2, bf16[256,4096]{1,0:T(8,128)(2,1)S(1)} %copy-done.3, bf16[256,2048]{1,0:T(8,128)(2,1)S(1)} %get-tuple-element.58.m_ref, bf16[256,2048]{1,0:T(8,128)(2,1)S(1)} %collective-permute-done.24.o_ref, ...), custom_call_target="tpu_custom_call" | custom-call | flops 10485760000 | bytes 524288000 | tf_op jit(solution)/shard_map/pallas_call | solution.py:90
  120.1 2.5 %shard_map.102 = (bf16[256,4096]{1,0:T(8,128)(2,1)}, bf16[256,4096]{1,0:T(8,128)(2,1)}) custom-call(bf16[256,4096]{1,0:T(8,128)(2,1)S(1)} %copy-done.2, bf16[256,4096]{1,0:T(8,128)(2,1)S(1)} %copy-done.3, bf16[256,2048]{1,0:T(8,128)(2,1)S(1)} %get-tuple-element.56.m_ref, ...), custom_call_target="tpu_custom_call", output_to_operand_aliasing={{0}: (4, {}), {1}: (5, {})} | custom-call | flops 10485760000 | bytes 524288000 | tf_op jit(solution)/shard_map/pallas_call | solution.py:90
  (27 shorter events, 0.2 us)
Async XLA Ops:
  0.6 8.2 %copy-start = (s32[128,4096]{1,0:T(8,128)S(1)}, s32[128,4096]{1,0:T(8,128)}, u32[]{:S(2)}) copy-start(s32[128,4096]{1,0:T(8,128)} %refs_16_.1) | copy-start | bytes 6291460
  4.1 4.6 %collective-permute-start.2 = (bf16[256,4096]{1,0:T(8,128)(2,1)}, bf16[256,4096]{1,0:T(8,128)(2,1)}, u32[]{:S(2)}, u32[]{:S(2)}) collective-permute-start(bf16[256,4096]{1,0:T(8,128)(2,1)} %shard_map.84.h_ref), channel_id=1, source_target_pairs={{0,1},{1,0},{2,3},{3,2},{4,5},{5,4},{6,7},{7,6},{8,9},{9,8},{10,11... | collective-permute-start | bytes 6291464 | tf_op jit(solution)/shard_map/ppermute | solution.py:559
  4.7 15.4 %collective-permute-start.1 = (bf16[256,1024]{1,0:T(8,128)(2,1)}, bf16[256,1024]{1,0:T(8,128)(2,1)S(1)}, u32[]{:S(2)}, u32[]{:S(2)}) collective-permute-start(bf16[256,1024]{1,0:T(8,128)(2,1)} %refs_4_.3), channel_id=1, source_target_pairs={{4,0},{8,4},{12,8},{14,12},{10,14},{6,10},{2,6},{0,2},{5,1},{9,5},... | collective-permute-start | bytes 1572872 | tf_op jit(solution)/shard_map/ppermute | solution.py:565
  7.2 14.2 %collective-permute-start = (bf16[256,1024]{1,0:T(8,128)(2,1)}, bf16[256,1024]{1,0:T(8,128)(2,1)S(1)}, u32[]{:S(2)}, u32[]{:S(2)}) collective-permute-start(bf16[256,1024]{1,0:T(8,128)(2,1)} %refs_4_.3), channel_id=1, source_target_pairs={{0,4},{4,8},{8,12},{12,14},{14,10},{10,6},{6,2},{2,0},{1,5},{5,9},... | collective-permute-start | bytes 1572872 | tf_op jit(solution)/shard_map/ppermute | solution.py:562
  8.8 1.6 %copy-start.1 = (bf16[256,4096]{1,0:T(8,128)(2,1)S(1)}, bf16[256,4096]{1,0:T(8,128)(2,1)}, u32[]{:S(2)}) copy-start(bf16[256,4096]{1,0:T(8,128)(2,1)} %shard_map.84.h_ref) | copy-start | bytes 6291460
  21.4 15.2 %collective-permute-start.3 = (bf16[256,1024]{1,0:T(8,128)(2,1)S(1)}, bf16[256,1024]{1,0:T(8,128)(2,1)S(1)}, u32[]{:S(2)}, u32[]{:S(2)}) collective-permute-start(bf16[256,1024]{1,0:T(8,128)(2,1)S(1)} %get-tuple-element.35.refs_0_.refs_3_.refs_15_.refs_7_), channel_id=1, source_target_pairs={{0,4},{4,8},{8,12},{12,14},{14,10},{10,6},{6,2},{2,0},{1,5},{5,9},... | collective-permute-start | bytes 1572872 | tf_op jit(solution)/shard_map/ppermute | solution.py:562
  21.8 14.9 %collective-permute-start.4 = (bf16[256,1024]{1,0:T(8,128)(2,1)S(1)}, bf16[256,1024]{1,0:T(8,128)(2,1)S(1)}, u32[]{:S(2)}, u32[]{:S(2)}) collective-permute-start(bf16[256,1024]{1,0:T(8,128)(2,1)S(1)} %get-tuple-element.36.refs_1_.refs_2_.refs_6_.refs_18_.refs_10_), channel_id=1, source_target_pairs={{4,0},{8,4},{12,8},{14,12},{10,14},{6,10},{2,6},{0,2},{5,1},{9,5},... | collective-permute-start | bytes 1572872 | tf_op jit(solution)/shard_map/ppermute | solution.py:565
  23.5 22.6 %collective-permute-start.7 = (bf16[256,1024]{1,0:T(8,128)(2,1)S(1)}, bf16[256,1024]{1,0:T(8,128)(2,1)S(1)}, u32[]{:S(2)}, u32[]{:S(2)}) collective-permute-start(bf16[256,1024]{1,0:T(8,128)(2,1)S(1)} %get-tuple-element.40), channel_id=1, source_target_pairs={{0,1},{1,0},{2,3},{3,2},{4,5},{5,4},{6,7},{7,6},{8,9},{9,8},{10,11... | collective-permute-start | bytes 1572872 | tf_op jit(solution)/shard_map/ppermute | solution.py:559
  36.1 23.6 %collective-permute-start.13 = (bf16[512,1024]{1,0:T(8,128)(2,1)S(1)}, bf16[512,1024]{1,0:T(8,128)(2,1)S(1)}, u32[]{:S(2)}, u32[]{:S(2)}) collective-permute-start(bf16[512,1024]{1,0:T(8,128)(2,1)S(1)} %get-tuple-element.46), channel_id=1, source_target_pairs={{0,1},{1,0},{2,3},{3,2},{4,5},{5,4},{6,7},{7,6},{8,9},{9,8},{10,11... | collective-permute-start | bytes 3145736 | tf_op jit(solution)/shard_map/ppermute | solution.py:559
  36.7 19.6 %collective-permute-start.5 = (bf16[256,1024]{1,0:T(8,128)(2,1)S(1)}, bf16[256,1024]{1,0:T(8,128)(2,1)S(1)}, u32[]{:S(2)}, u32[]{:S(2)}) collective-permute-start(bf16[256,1024]{1,0:T(8,128)(2,1)S(1)} %get-tuple-element.38.refs_0_.refs_3_.refs_21_.refs_13_), channel_id=1, source_target_pairs={{0,4},{4,8},{8,12},{12,14},{14,10},{10,6},{6,2},{2,0},{1,5},{5,9},... | collective-permute-start | bytes 1572872 | tf_op jit(solution)/shard_map/ppermute | solution.py:562
  37.0 19.3 %collective-permute-start.6 = (bf16[256,1024]{1,0:T(8,128)(2,1)S(1)}, bf16[256,1024]{1,0:T(8,128)(2,1)S(1)}, u32[]{:S(2)}, u32[]{:S(2)}) collective-permute-start(bf16[256,1024]{1,0:T(8,128)(2,1)S(1)} %get-tuple-element.39.refs_1_.refs_2_.refs_20_.refs_12_), channel_id=1, source_target_pairs={{4,0},{8,4},{12,8},{14,12},{10,14},{6,10},{2,6},{0,2},{5,1},{9,5},... | collective-permute-start | bytes 1572872 | tf_op jit(solution)/shard_map/ppermute | solution.py:565
  38.9 8.9 %collective-permute-start.10 = (bf16[256,1024]{1,0:T(8,128)(2,1)S(1)}, bf16[256,1024]{1,0:T(8,128)(2,1)S(1)}, u32[]{:S(2)}, u32[]{:S(2)}) collective-permute-start(bf16[256,1024]{1,0:T(8,128)(2,1)S(1)} %shard_map.91), channel_id=1, source_target_pairs={{0,1},{1,0},{2,3},{3,2},{4,5},{5,4},{6,7},{7,6},{8,9},{9,8},{10,11... | collective-permute-start | bytes 1572872 | tf_op jit(solution)/shard_map/ppermute | solution.py:559
  46.2 10.1 %collective-permute-start.9 = (bf16[128,1024]{1,0:T(8,128)(2,1)S(1)}, bf16[128,1024]{1,0:T(8,128)(2,1)S(1)}, u32[]{:S(2)}, u32[]{:S(2)}) collective-permute-start(bf16[128,1024]{1,0:T(8,128)(2,1)S(1)} %get-tuple-element.70), channel_id=1, source_target_pairs={{4,0},{8,4},{12,8},{14,12},{10,14},{6,10},{2,6},{0,2},{5,1},{9,5},... | collective-permute-start | bytes 786440 | tf_op jit(solution)/shard_map/ppermute | solution.py:565
  47.9 8.4 %collective-permute-start.8 = (bf16[128,1024]{1,0:T(8,128)(2,1)S(1)}, bf16[128,1024]{1,0:T(8,128)(2,1)S(1)}, u32[]{:S(2)}, u32[]{:S(2)}) collective-permute-start(bf16[128,1024]{1,0:T(8,128)(2,1)S(1)} %get-tuple-element.71), channel_id=1, source_target_pairs={{0,4},{4,8},{8,12},{12,14},{14,10},{10,6},{6,2},{2,0},{1,5},{5,9},... | collective-permute-start | bytes 786440 | tf_op jit(solution)/shard_map/ppermute | solution.py:562
  57.0 4.9 %collective-permute-start.16 = (bf16[512,1024]{1,0:T(8,128)(2,1)S(1)}, bf16[512,1024]{1,0:T(8,128)(2,1)S(1)}, u32[]{:S(2)}, u32[]{:S(2)}) collective-permute-start(bf16[512,1024]{1,0:T(8,128)(2,1)S(1)} %shard_map.94), channel_id=1, source_target_pairs={{0,1},{1,0},{2,3},{3,2},{4,5},{5,4},{6,7},{7,6},{8,9},{9,8},{10,11... | collective-permute-start | bytes 3145736 | tf_op jit(solution)/shard_map/ppermute | solution.py:559
  57.1 21.8 %collective-permute-start.17 = (bf16[256,1024]{1,0:T(8,128)(2,1)S(1)}, bf16[256,1024]{1,0:T(8,128)(2,1)S(1)}, u32[]{:S(2)}, u32[]{:S(2)}) collective-permute-start(bf16[256,1024]{1,0:T(8,128)(2,1)S(1)} %get-tuple-element.49), channel_id=1, source_target_pairs={{0,1},{1,0},{2,3},{3,2},{4,5},{5,4},{6,7},{7,6},{8,9},{9,8},{10,11... | collective-permute-start | bytes 1572872 | tf_op jit(solution)/shard_map/ppermute | solution.py:559
  57.6 18.5 %collective-permute-start.12 = (bf16[128,1024]{1,0:T(8,128)(2,1)S(1)}, bf16[128,1024]{1,0:T(8,128)(2,1)S(1)}, u32[]{:S(2)}, u32[]{:S(2)}) collective-permute-start(bf16[128,1024]{1,0:T(8,128)(2,1)S(1)} %slice.27), channel_id=1, source_target_pairs={{4,0},{8,4},{12,8},{14,12},{10,14},{6,10},{2,6},{0,2},{5,1},{9,5},... | collective-permute-start | bytes 786440 | tf_op jit(solution)/shard_map/ppermute | solution.py:565
  59.3 16.8 %collective-permute-start.11 = (bf16[128,1024]{1,0:T(8,128)(2,1)S(1)}, bf16[128,1024]{1,0:T(8,128)(2,1)S(1)}, u32[]{:S(2)}, u32[]{:S(2)}) collective-permute-start(bf16[128,1024]{1,0:T(8,128)(2,1)S(1)} %slice.26), channel_id=1, source_target_pairs={{0,4},{4,8},{8,12},{12,14},{14,10},{10,6},{6,2},{2,0},{1,5},{5,9},... | collective-permute-start | bytes 786440 | tf_op jit(solution)/shard_map/ppermute | solution.py:562
  60.2 17.0 %collective-permute-start.15 = (bf16[256,1024]{1,0:T(8,128)(2,1)S(1)}, bf16[256,1024]{1,0:T(8,128)(2,1)S(1)}, u32[]{:S(2)}, u32[]{:S(2)}) collective-permute-start(bf16[256,1024]{1,0:T(8,128)(2,1)S(1)} %get-tuple-element.66.refs_11_), channel_id=1, source_target_pairs={{4,0},{8,4},{12,8},{14,12},{10,14},{6,10},{2,6},{0,2},{5,1},{9,5},... | collective-permute-start | bytes 1572872 | tf_op jit(solution)/shard_map/ppermute | solution.py:565
  61.9 16.6 %collective-permute-start.14 = (bf16[256,1024]{1,0:T(8,128)(2,1)S(1)}, bf16[256,1024]{1,0:T(8,128)(2,1)S(1)}, u32[]{:S(2)}, u32[]{:S(2)}) collective-permute-start(bf16[256,1024]{1,0:T(8,128)(2,1)S(1)} %get-tuple-element.67.refs_10_), channel_id=1, source_target_pairs={{0,4},{4,8},{8,12},{12,14},{14,10},{10,6},{6,2},{2,0},{1,5},{5,9},... | collective-permute-start | bytes 1572872 | tf_op jit(solution)/shard_map/ppermute | solution.py:562
  78.6 2.8 %collective-permute-start.20 = (bf16[256,1024]{1,0:T(8,128)(2,1)S(1)}, bf16[256,1024]{1,0:T(8,128)(2,1)S(1)}, u32[]{:S(2)}, u32[]{:S(2)}) collective-permute-start(bf16[256,1024]{1,0:T(8,128)(2,1)S(1)} %shard_map.97), channel_id=1, source_target_pairs={{0,1},{1,0},{2,3},{3,2},{4,5},{5,4},{6,7},{7,6},{8,9},{9,8},{10,11... | collective-permute-start | bytes 1572872 | tf_op jit(solution)/shard_map/ppermute | solution.py:559
  79.3 21.2 %collective-permute-start.19 = (bf16[256,1024]{1,0:T(8,128)(2,1)S(1)}, bf16[256,1024]{1,0:T(8,128)(2,1)S(1)}, u32[]{:S(2)}, u32[]{:S(2)}) collective-permute-start(bf16[256,1024]{1,0:T(8,128)(2,1)S(1)} %get-tuple-element.68.refs_26_), channel_id=1, source_target_pairs={{4,0},{8,4},{12,8},{14,12},{10,14},{6,10},{2,6},{0,2},{5,1},{9,5},... | collective-permute-start | bytes 1572872 | tf_op jit(solution)/shard_map/ppermute | solution.py:565
  81.0 19.6 %collective-permute-start.18 = (bf16[256,1024]{1,0:T(8,128)(2,1)S(1)}, bf16[256,1024]{1,0:T(8,128)(2,1)S(1)}, u32[]{:S(2)}, u32[]{:S(2)}) collective-permute-start(bf16[256,1024]{1,0:T(8,128)(2,1)S(1)} %get-tuple-element.69.refs_25_), channel_id=1, source_target_pairs={{0,4},{4,8},{8,12},{12,14},{14,10},{10,6},{6,2},{2,0},{1,5},{5,9},... | collective-permute-start | bytes 1572872 | tf_op jit(solution)/shard_map/ppermute | solution.py:562
  100.4 16.4 %collective-permute-start.24 = (bf16[256,2048]{1,0:T(8,128)(2,1)S(1)}, bf16[256,2048]{1,0:T(8,128)(2,1)S(1)}, u32[]{:S(2)}, u32[]{:S(2)}) collective-permute-start(bf16[256,2048]{1,0:T(8,128)(2,1)S(1)} %get-tuple-element.53.refs_2_), channel_id=1, source_target_pairs={{0,1},{1,0},{2,3},{3,2},{4,5},{5,4},{6,7},{7,6},{8,9},{9,8},{10,11... | collective-permute-start | bytes 3145736 | tf_op jit(solution)/shard_map/ppermute | solution.py:559
  101.2 14.9 %collective-permute-start.21 = (bf16[256,1024]{1,0:T(8,128)(2,1)S(1)}, bf16[256,1024]{1,0:T(8,128)(2,1)S(1)}, u32[]{:S(2)}, u32[]{:S(2)}) collective-permute-start(bf16[256,1024]{1,0:T(8,128)(2,1)S(1)} %get-tuple-element.64.refs_17_), channel_id=1, source_target_pairs={{0,4},{4,8},{8,12},{12,14},{14,10},{10,6},{6,2},{2,0},{1,5},{5,9},... | collective-permute-start | bytes 1572872 | tf_op jit(solution)/shard_map/ppermute | solution.py:562
  102.4 14.1 %collective-permute-start.22 = (bf16[256,1024]{1,0:T(8,128)(2,1)S(1)}, bf16[256,1024]{1,0:T(8,128)(2,1)S(1)}, u32[]{:S(2)}, u32[]{:S(2)}) collective-permute-start(bf16[256,1024]{1,0:T(8,128)(2,1)S(1)} %get-tuple-element.65.refs_18_), channel_id=1, source_target_pairs={{4,0},{8,4},{12,8},{14,12},{10,14},{6,10},{2,6},{0,2},{5,1},{9,5},... | collective-permute-start | bytes 1572872 | tf_op jit(solution)/shard_map/ppermute | solution.py:565
  103.3 13.6 %copy-start.3 = (bf16[256,4096]{1,0:T(8,128)(2,1)S(1)}, bf16[256,4096]{1,0:T(8,128)(2,1)}, u32[]{:S(2)}) copy-start(bf16[256,4096]{1,0:T(8,128)(2,1)} %u_ref.5) | copy-start | bytes 6291460
  116.0 1.6 %copy-start.2 = (bf16[256,4096]{1,0:T(8,128)(2,1)S(1)}, bf16[256,4096]{1,0:T(8,128)(2,1)}, u32[]{:S(2)}) copy-start(bf16[256,4096]{1,0:T(8,128)(2,1)} %g_ref.5) | copy-start | bytes 6291460
  116.0 4.1 %collective-permute-start.23 = (bf16[256,2048]{1,0:T(8,128)(2,1)S(1)}, bf16[256,2048]{1,0:T(8,128)(2,1)S(1)}, u32[]{:S(2)}, u32[]{:S(2)}) collective-permute-start(bf16[256,2048]{1,0:T(8,128)(2,1)S(1)} %get-tuple-element.57.refs_0_), channel_id=1, source_target_pairs={{0,1},{1,0},{2,3},{3,2},{4,5},{5,4},{6,7},{7,6},{8,9},{9,8},{10,11... | collective-permute-start | bytes 3145736 | tf_op jit(solution)/shard_map/ppermute | solution.py:559
  116.8 3.2 %copy-start.4 = (bf16[256,1024]{1,0:T(8,128)(2,1)}, bf16[256,1024]{1,0:T(8,128)(2,1)S(1)}, u32[]{:S(2)}) copy-start(bf16[256,1024]{1,0:T(8,128)(2,1)S(1)} %add_convert_fusion.refs_2_) | copy-start | bytes 1572868
